TPU v7x, 256 devices: a whole 4x4x8 slice. The times are simulated.
256 devices in a mesh: seq: 8 (over y, z_lo), res: 32 (over z_hi, x, core).
Axes of the slice: x: 4, y: 4, z: 8 (z_hi: 4, z_lo: 2; z = z_hi * 2 + z_lo), core: 2. Of those that a mesh axis runs over, the one named last changes fastest.
Arguments:
- homolog_stack: bfloat16 [256, 512, 256], P('seq', 'res'), may hold values from -6 to 6
- presence_flags: int32 [256, 512], P('seq', 'res'), may hold values from 0 to 1, as said below
- normalizer_scaling: float32 [256], replicated, may hold values from 0.25 to 1.75
- normalizer_offset: float32 [256], replicated, may hold values from -1.5 to 1.5
- first_factor_matrix: bfloat16 [256, 32], replicated, may hold values from -0.375 to 0.375
- first_factor_offset: float32 [32], replicated, may hold values from -2.5 to 2.5
- second_factor_matrix: bfloat16 [256, 32], replicated, may hold values from -0.375 to 0.375
- second_factor_offset: float32 [32], replicated, may hold values from -2.5 to 2.5
- final_mapping_matrix: bfloat16 [1024, 128], replicated, may hold values from -2.5 to 2.5
- coupling_delta_cotangent: bfloat16 [512, 512, 128], P('res', 'seq'), may hold values from -6 to 6
Outputs:
- pair: bfloat16 [512, 512, 128], P('res', 'seq')
- alignment_gradient: bfloat16 [256, 512, 256], P('seq', 'res')
Inputs may be any that keep to these rules, and one draw needn't show every extreme that they name: Row 0 of presence_flags (the target sequence) is all ones.
All inputs are finite; a program needn't handle non-finite values.
Results may differ from a plain program's by a relative error of at most 0.017.
Values may be sent and summed in bfloat16 or wider, within the bound.
A program may use at most 64 MiB of HBM per device.

v0:
```python
import jax
import jax.numpy as jnp
from jax import lax
from jax.sharding import PartitionSpec as P


def homolog_embedding(
    homolog_cells,
    flag_cells,
    normalizer_scaling,
    normalizer_offset,
    first_factor_matrix,
    first_factor_offset,
    second_factor_matrix,
    second_factor_offset,
):
    middle_product = jnp.mean(homolog_cells, axis=-1, keepdims=True)
    mean_removed = homolog_cells - middle_product
    spread = jnp.mean(mean_removed * mean_removed, axis=-1, keepdims=True)
    normed = mean_removed * lax.rsqrt(spread + 1e-05) * normalizer_scaling + normalizer_offset
    first_factor_hidden = (
        jnp.einsum(
            "sic,cd->sid",
            normed,
            first_factor_matrix.astype(jnp.float32),
            precision=lax.Precision.HIGHEST,
        )
        + first_factor_offset
    )
    second_factor_hidden = (
        jnp.einsum(
            "sic,cd->sid",
            normed,
            second_factor_matrix.astype(jnp.float32),
            precision=lax.Precision.HIGHEST,
        )
        + second_factor_offset
    )
    return (
        flag_cells[:, :, None] * first_factor_hidden,
        flag_cells[:, :, None] * second_factor_hidden,
    )


def body(
    homolog_stack,
    presence_flags,
    normalizer_scaling,
    normalizer_offset,
    first_factor_matrix,
    first_factor_offset,
    second_factor_matrix,
    second_factor_offset,
    final_mapping_matrix,
    coupling_delta_cotangent,
):
    local_homolog_count, local_position_count, ignored_element = homolog_stack.shape
    proj = first_factor_matrix.shape[1]
    width = final_mapping_matrix.shape[1]
    flag_cells = presence_flags.astype(jnp.float32)

    def widened_source(numeric_array):
        return homolog_embedding(
            numeric_array,
            flag_cells,
            normalizer_scaling,
            normalizer_offset,
            first_factor_matrix,
            first_factor_offset,
            second_factor_matrix,
            second_factor_offset,
        )

    (first_factor_hidden, second_factor_hidden), reverse_rule = jax.vjp(
        widened_source, homolog_stack.astype(jnp.float32)
    )
    left_t = jnp.transpose(first_factor_hidden.astype(jnp.bfloat16), (1, 0, 2))
    second_factor_lines = jnp.transpose(
        second_factor_hidden.astype(jnp.bfloat16), (1, 0, 2)
    ).reshape(local_position_count, local_homolog_count * proj)
    mask_rows = jnp.transpose(flag_cells).astype(jnp.bfloat16)
    flattened_matrix = final_mapping_matrix.reshape(proj, proj * width)
    collapsed_sum = jnp.einsum(
        "isc,cq->isq", left_t, flattened_matrix, preferred_element_type=jnp.float32
    )
    collapsed_sum = collapsed_sum.astype(jnp.bfloat16).reshape(
        local_position_count, local_homolog_count * proj, width
    )
    slab, slab_mask = (
        lax.all_gather(second_factor_lines, "res", axis=0, tiled=True),
        lax.all_gather(mask_rows, "res", axis=0, tiled=True),
    )
    numer = jnp.einsum("jp,ipk->ijk", slab, collapsed_sum, preferred_element_type=jnp.float32)
    counts = jnp.dot(mask_rows, jnp.transpose(slab_mask), preferred_element_type=jnp.float32)
    numer, counts = (
        lax.psum_scatter(numer.astype(jnp.bfloat16), "seq", scatter_dimension=1, tiled=True).astype(
            jnp.float32
        ),
        lax.psum_scatter(
            counts.astype(jnp.bfloat16), "seq", scatter_dimension=1, tiled=True
        ).astype(jnp.float32),
    )
    denom = counts + 0.001
    pair = (numer / denom[:, :, None]).astype(jnp.bfloat16)
    scaled = (coupling_delta_cotangent.astype(jnp.float32) / denom[:, :, None]).astype(jnp.bfloat16)
    scaled_all = lax.all_gather(scaled, "seq", axis=1, tiled=True)
    traversed_state = jnp.einsum(
        "jp,ijk->ipk", slab, scaled_all, preferred_element_type=jnp.float32
    ).astype(jnp.bfloat16)
    first_factor_cotangent_value = jnp.einsum(
        "nlw,ow->nlo",
        traversed_state.reshape(local_position_count, local_homolog_count, proj * width),
        flattened_matrix,
        preferred_element_type=jnp.float32,
    )
    second_factor_cotangent_value = lax.psum_scatter(
        jnp.einsum(
            "ijk,ipk->jp", scaled_all, collapsed_sum, preferred_element_type=jnp.float32
        ).astype(jnp.bfloat16),
        "res",
        scatter_dimension=0,
        tiled=True,
    ).astype(jnp.float32)
    second_factor_cotangent_value = second_factor_cotangent_value.reshape(
        local_position_count, local_homolog_count, proj
    )
    alignment_gradient = reverse_rule(
        (
            jnp.transpose(first_factor_cotangent_value, (1, 0, 2)),
            jnp.transpose(second_factor_cotangent_value, (1, 0, 2)),
        )
    )[0]
    return (pair, alignment_gradient.astype(jnp.bfloat16))


def solution(mesh):
    return jax.shard_map(
        body,
        mesh=mesh,
        in_specs=(
            P("seq", "res", None),
            P("seq", "res"),
            P(),
            P(),
            P(),
            P(),
            P(),
            P(),
            P(),
            P("res", "seq", None),
        ),
        out_specs=(P("res", "seq", None), P("seq", "res", None)),
        check_vma=False,
    )
```

profile of v0, /device:TPU:32, one launch (start us, length us, event | category | flops | bytes accessed | tf_op | source)
XLA Modules:
  0.0 312.7 jit_solution(2841972575116098016)
XLA Ops:
  8.1 1.1 convert_reduce_fusion
  9.2 1.2 fusion.19
  10.4 0.7 fusion.43
  11.2 1.5 fusion.12
  12.7 0.8 reshape.52
  13.6 46.8 %all_gather.10 = bf16[512,32]{1,0:T(8,128)(2,1)S(1)} all-gather(bf16[16,32]{1,0:T(8,128)(2,1)S(1)} %get-tuple-element.12), channel_id=1, replica_groups=mesh['seq'=8,'res'=32] {'res'}, dimensions={0}, use_global_device_ids=true | all-gather | bytes 33792 | tf_op jit(solution)/shard_map/all_gather | solution.py:91
  60.5 0.8 copy.46
  61.3 1.1 reshape.57
  62.4 1.5 fusion.11
  63.9 3.2 %convolution_convert_fusion = bf16[16,32,4096]{2,1,0:T(8,128)(2,1)} fusion(bf16[32,4096,1]{1,0,2:T(8,128)(2,1)S(1)} %reshape.57, bf16[16,32,32]{2,0,1:T(8,128)(2,1)S(1)} %fusion.11), kind=kOutput, calls=%fused_computation | convolution fusion | flops 136314880 | bytes 4489216 | tf_op jit(solution)/shard_map/isc,cq->isq/dot_general | solution.py:83
  67.1 7.4 %reshape.51 = bf16[16,1024,128]{2,1,0:T(8,128)(2,1)} reshape(bf16[16,32,4096]{2,1,0:T(8,128)(2,1)} %convolution_convert_fusion) | data formatting | bytes 8388608 | tf_op jit(solution)/shard_map/reshape | solution.py:86
  74.5 4.9 %convert_bitcast_fusion.1 = bf16[16,512,128]{1,2,0:T(8,128)(2,1)S(1)} fusion(bf16[16,1024,128]{2,1,0:T(8,128)(2,1)} %reshape.51, bf16[512,1024]{1,0:T(8,128)(2,1)} %all-gather.3.cloned.1.call-done), kind=kOutput, calls=%fused_computation.3 | convolution fusion | flops 2148532224 | bytes 7340032 | tf_op jit(solution)/shard_map/jp,ipk->ijk/dot_general | solution.py:93
  79.4 3.1 copy.36
  82.5 10.6 %reduce-scatter.10.cloned.1.call-done = bf16[64,16]{1,0:T(8,128)(2,1)} async-done(((bf16[512,16]{1,0:T(8,128)(2,1)}), bf16[64,16]{1,0:T(8,128)(2,1)}) %reduce-scatter.10.cloned.1.call-update) | async-done | bytes 2064
  93.1 0.8 copy.47
  94.0 55.8 %reduce-scatter.6.cloned.1.call-done = bf16[16,64,128]{2,0,1:T(8,128)(2,1)} async-done(((bf16[16,512,128]{2,0,1:T(8,128)(2,1)}), bf16[16,64,128]{2,0,1:T(8,128)(2,1)}) %reduce-scatter.6.cloned.1.call-update) | async-done | bytes 262160 | tf_op jit(solution)/shard_map/reduce_scatter | solution.py:96
  149.8 1.9 divide_convert_fusion
  151.7 0.2 reduce-scatter.8.cloned.1.call-start
  151.9 54.1 %all-gather.5.cloned.1.call-done = bf16[16,512,128]{2,0,1:T(8,128)(2,1)} async-done(((bf16[16,64,128]{2,0,1:T(8,128)(2,1)}), bf16[16,512,128]{2,0,1:T(8,128)(2,1)}) %all-gather.5.cloned.1.call-update) | async-done | bytes 2097168 | tf_op jit(solution)/shard_map/all_gather | solution.py:106
  206.1 6.1 %bitcast_convert_fusion = bf16[512,1024]{1,0:T(8,128)(2,1)} fusion(bf16[16,1024,128]{2,1,0:T(8,128)(2,1)} %reshape.51, bf16[16,512,128]{2,0,1:T(8,128)(2,1)} %all-gather.5.cloned.1.call-done), kind=kOutput, calls=%fused_computation.2 | convolution fusion | flops 2148007936 | bytes 7340032 | tf_op jit(solution)/shard_map/ijk,ipk->jp/dot_general | solution.py:117
  212.2 0.8 copy.44
  213.0 6.0 %convert_bitcast_fusion = bf16[16,1024,128]{1,2,0:T(8,128)(2,1)} fusion(bf16[16,512,128]{2,0,1:T(8,128)(2,1)} %all-gather.5.cloned.1.call-done, bf16[512,1024]{1,0:T(8,128)(2,1)S(1)} %copy-done.5), kind=kOutput, calls=%fused_computation.1 | convolution fusion | flops 2149580800 | bytes 7340032 | tf_op jit(solution)/shard_map/jp,ijk->ipk/dot_general | solution.py:107
  219.0 6.4 %copy.42 = bf16[16,1024,128]{2,1,0:T(8,128)(2,1)} copy(bf16[16,1024,128]{1,2,0:T(8,128)(2,1)} %convert_bitcast_fusion) | data formatting | bytes 8388608 | tf_op jit(solution)/shard_map/convert_element_type | solution.py:109
  225.4 7.3 %reshape.54 = bf16[16,32,4096]{2,1,0:T(8,128)(2,1)} reshape(bf16[16,1024,128]{2,1,0:T(8,128)(2,1)} %copy.42) | data formatting | bytes 8388608 | tf_op jit(solution)/shard_map/reshape | solution.py:112
  232.7 3.5 %fusion.6 = f32[32,16,32]{2,0,1:T(8,128)S(1)} fusion(bf16[16,32,4096]{2,1,0:T(8,128)(2,1)} %reshape.54, bf16[32,4096,1]{1,0,2:T(8,128)(2,1)S(1)} %reshape.57, f32[32,16]{0,1:T(8,128)S(1)} %get-tuple-element.10), kind=kOutput, calls=%fused_computation.10 | convolution fusion | flops 134234112 | bytes 4524032 | tf_op jit(solution)/shard_map/nlw,ow->nlo/dot_general | solution.py:110
  236.2 65.3 %reduce-scatter.8.cloned.1.call-done = bf16[16,1024]{1,0:T(8,128)(2,1)} async-done(((bf16[512,1024]{1,0:T(8,128)(2,1)}), bf16[16,1024]{1,0:T(8,128)(2,1)}) %reduce-scatter.8.cloned.1.call-update) | async-done | bytes 32784 | tf_op jit(solution)/shard_map/reduce_scatter | solution.py:116
  301.5 0.9 reshape.55
  302.4 0.1 bitcast_multiply_fusion
  302.6 0.5 fusion.26
  303.1 0.6 fusion.24
  303.6 0.4 fusion.36
  304.0 1.0 add_convert_fusion
  (31 shorter events, 0.7 us)
Async XLA Ops:
  8.0 54.4 %copy-start = (bf16[256,32]{0,1:T(8,128)(2,1)S(1)}, bf16[256,32]{0,1:T(8,128)(2,1)}, u32[]{:S(2)}) copy-start(bf16[256,32]{0,1:T(8,128)(2,1)} %param.14) | copy-start | bytes 49156
  8.0 66.5 %all-gather.3.cloned.1.call-start = ((), (), s32[]{:S(2)}) async-start(), calls=%async_computation.3 | async-start | bytes 1081344 | tf_op jit(solution)/shard_map/all_gather | solution.py:90
  13.5 79.6 %reduce-scatter.10.cloned.1.call-start = ((), (), s32[]{:S(2)}) async-start(), calls=%async_computation.7 | async-start | bytes 147456
  61.3 88.5 %reduce-scatter.6.cloned.1.call-start = ((), (), s32[]{:S(2)}) async-start(), calls=%async_computation.4 | async-start | bytes 2359296 | tf_op jit(solution)/shard_map/reduce_scatter | solution.py:96
  79.4 70.4 %copy-start.2 = (bf16[16,64,128]{2,1,0:T(8,128)(2,1)S(1)}, bf16[16,64,128]{2,1,0:T(8,128)(2,1)}, u32[]{:S(2)}) copy-start(bf16[16,64,128]{2,1,0:T(8,128)(2,1)} %param.19) | copy-start | bytes 786436
  82.5 123.6 %all-gather.5.cloned.1.call-start = ((), (), s32[]{:S(2)}) async-start(), calls=%async_computation.5 | async-start | bytes 2359296 | tf_op jit(solution)/shard_map/all_gather | solution.py:106
  151.7 61.3 %copy-start.5 = (bf16[512,1024]{1,0:T(8,128)(2,1)S(1)}, bf16[512,1024]{1,0:T(8,128)(2,1)}, u32[]{:S(2)}) copy-start(bf16[512,1024]{1,0:T(8,128)(2,1)} %all-gather.3.cloned.1.call-done) | copy-start | bytes 3145732
  151.7 149.8 %reduce-scatter.8.cloned.1.call-start = ((), (), s32[]{:S(2)}) async-start(), calls=%async_computation.6 | async-start | bytes 1081344 | tf_op jit(solution)/shard_map/reduce_scatter | solution.py:116
  232.7 69.9 %copy-start.3 = (bf16[256,32]{0,1:T(8,128)(2,1)S(1)}, bf16[256,32]{0,1:T(8,128)(2,1)}, u32[]{:S(2)}) copy-start(bf16[256,32]{0,1:T(8,128)(2,1)} %param.16) | copy-start | bytes 49156
  232.7 70.3 %copy-start.1 = (bf16[32,16,256]{2,1,0:T(8,128)(2,1)S(1)}, bf16[32,16,256]{2,1,0:T(8,128)(2,1)}, u32[]{:S(2)}) copy-start(bf16[32,16,256]{2,1,0:T(8,128)(2,1)} %param.10) | copy-start | bytes 786436
  232.7 70.3 %copy-start.4 = (f32[256]{0:T(256)S(1)}, f32[256]{0:T(256)}, u32[]{:S(2)}) copy-start(f32[256]{0:T(256)} %param.12) | copy-start | bytes 3076
Sparse Core Ops, SparseCore 0:
  13.6 53.2 all-gather.2
  212.4 89.1 reduce-scatter.7
Sparse Core Ops, SparseCore 1:
  61.4 31.7 reduce-scatter.9
  95.7 54.0 reduce-scatter.5
  152.1 53.9 all-gather.4
where the time goes:
time: 315 us; the launch traced here: 313 us
  waiting for transfers between devices  186 us (59%)
  blocking collectives  46.8 us (15%)
  local copies, waits for them, and re-layouts  29.5 us (9%)
  matrix products  27.8 us (9%)
  between operations  15.8 us (5%)
  other arithmetic  6.47 us (2%)
    reduce_scatter x1, waiting for transfers between devices, body(): lax.psum_scatter(jnp.einsum('ijk,ipk->jp', scaled_all, collapsed_sum, pre...  65.3 us
    reduce_scatter x1, waiting for transfers between devices, body(): lax.psum_scatter(numer.astype(jnp.bfloat16), 'seq', scatter_dimension=1,...  55.8 us
    all_gather x1, waiting for transfers between devices, body(): scaled_all = lax.all_gather(scaled, 'seq', axis=1, tiled=True)  54.1 us
    all_gather x1, blocking collectives, body(): lax.all_gather(mask_rows, 'res', axis=0, tiled=True)  46.8 us
    unnamed x6, waiting for transfers between devices  10.7 us
    reshape x1, local copies, waits for them, and re-layouts, body(): collapsed_sum.astype(jnp.bfloat16)  7.38 us
    reshape x1, local copies, waits for them, and re-layouts, body(): traversed_state.reshape(local_position_count, local_homolog_count, proj *...  7.31 us
    convert_element_type x1, local copies, waits for them, and re-layouts, body(): traversed_state = jnp.einsum('jp,ijk->ipk', slab, scaled_all, preferred_e...  6.42 us
  transfers between devices with their start and end apart: 5, of which 4 were waited for; matrix products, arithmetic and copies ran while one was open for 15% of the time, Pallas kernels for 0%

commit v1 on v0

v1 whole, which is shorter than its diff:
```python
import jax
import jax.numpy as jnp
from jax import lax
from jax.experimental import pallas as pl
from jax.experimental.pallas import tpu as pltpu
from jax.sharding import PartitionSpec as P

F32 = jnp.float32
BF = jnp.bfloat16
MESH = pl.DeviceIdType.MESH


def dot(a, b, ca=1, cb=0):
    return lax.dot_general(a, b, (((ca,), (cb,)), ((), ())), preferred_element_type=F32)


def rem(a, n):
    return lax.rem(a, jnp.int32(n))


def div(a, n):
    return lax.div(a, jnp.int32(n))


def split(a):
    hi = a.astype(BF)
    return hi, (a - hi.astype(F32)).astype(BF)


def ones_where(condition):
    return jnp.where(condition, 1.0, 0.0)


def iota(shape, dim):
    return lax.broadcasted_iota(jnp.int32, shape, dim)


def swap_halves(a, b):
    low = iota(a.shape, 1) < 64
    return (
        jnp.where(low, a, pltpu.roll(b, 64, 1)),
        jnp.where(low, pltpu.roll(a, 64, 1), b),
    )


def kernel(
    x_ref, flag_ref, gain_ref, shift_ref, w1_ref, b1_ref, w2_ref, b2_ref, wm_ref, delta_ref,
    pair_ref, grad_ref,
    xhat_ref, rstd_ref, proj_ref, wf_ref, wec_ref, wt_ref, dt_ref, mask1_ref, mask2_ref, perm1_ref, perm2_ref,
    zbuf, lall, rall, left_ref, right_ref, tile_ref, d_ref, pt_ref,
    gsend, gcore, hsend, gx, ksend, gy, gz, lsend, lrecv, dn_ref,
    zs, zr, ys, yr, xs, xr, cs, cr, ls, lr,
    bzs, bzr, bys, byr, bxs, bxr, bcs, bcr, bls, blr,
):
    q = lax.axis_index("seq")
    r = lax.axis_index("res")
    y, zl = div(q, 2), rem(q, 2)
    zh, x, core = div(r, 8), rem(div(r, 2), 4), rem(r, 2)
    other = 1 - core

    def device(x_=x, y_=y, zh_=zh, zl_=zl, core_=core):
        return {"seq": y_ * 2 + zl_, "res": zh_ * 8 + x_ * 2 + core_}

    def crossed(x_):
        return rem(div(x_, 2) + zl, 2)

    def twin(x_):
        m = crossed(x_)
        return x_ + m * (3 - 2 * x_), rem(zl + m, 2)

    mine_crossed = crossed(x)
    tx, tzl = twin(x)

    def remote(src, dst, send, recv, where):
        return pltpu.make_async_remote_copy(
            src_ref=src, dst_ref=dst, send_sem=send, recv_sem=recv, device_id=where, device_id_type=MESH
        )

    barrier = pltpu.get_barrier_semaphore()

    def greet(where):
        pl.semaphore_signal(barrier, inc=1, device_id=where, device_id_type=MESH)

    for d in range(1, 4):
        greet(device(zh_=rem(zh + d, 4)))
        greet(device(x_=rem(x + d, 4)))
    greet(device(core_=other))
    for k in range(1, 8):
        greet(device(y_=rem(y + k // 2, 4), zl_=rem(zl + k % 2, 2)))

    @pl.when(mine_crossed == 1)
    def _():
        for t in range(4):
            greet(device(x_=tx, zl_=tzl, y_=jnp.int32(t)))

    xv = x_ref[...].astype(F32).reshape(512, 256)
    centred = xv - jnp.mean(xv, axis=-1, keepdims=True)
    rstd = lax.rsqrt(jnp.mean(centred * centred, axis=-1, keepdims=True) + 1e-5)
    xhat = centred * rstd
    xhat_ref[...] = xhat
    rstd_ref[...] = jnp.broadcast_to(rstd, (512, 128))
    hi, lo = split(xhat * gain_ref[...] + shift_ref[...])
    w = jnp.concatenate([w1_ref[...], w2_ref[...]], axis=1)
    bias = jnp.concatenate([b1_ref[...], b2_ref[...]], axis=1)
    proj_ref[:, 0:64] = dot(hi, w) + dot(lo, w) + bias

    rows, cols = iota((512, 512), 0), iota((512, 512), 1)
    perm1 = ones_where(((rows >> 5) == (cols & 15)) & ((rows & 31) == (cols >> 4))).astype(BF)
    perm1_ref[...] = perm1
    flags = flag_ref[...].astype(F32).astype(BF)
    mask1 = dot(flags, ones_where(iota((16, 512), 0) == (iota((16, 512), 1) >> 5)).astype(BF))
    mask2 = dot(flags, ones_where(iota((16, 512), 0) == (iota((16, 512), 1) & 15)).astype(BF))
    mask1_ref[...] = mask1
    mask2_ref[...] = mask2
    flags_t = dot(flags, ones_where(iota((32, 128), 0) == iota((32, 128), 1)).astype(BF), 0, 0).astype(BF)
    parts = [proj_ref[pl.ds(i, 32, stride=16), :] for i in range(16)]
    lw = (jnp.concatenate([p[:, 0:32] for p in parts], axis=1) * mask1).astype(BF)
    rw = jnp.concatenate([p[:, 32:64] for p in parts], axis=1).astype(BF)
    rw = (dot(rw, perm1) * mask2).astype(BF)
    for l in range(4):
        for h in range(2):
            lall[zl, y, 2 * l + h] = lw[16 * h : 16 * h + 16, 128 * l : 128 * l + 128]
            zbuf[zh, 2 * l + h] = rw[16 * h : 16 * h + 16, 128 * l : 128 * l + 128]
    lall[zl, y, 8] = flags_t
    zbuf[zh, 8] = flags_t

    pl.semaphore_wait(barrier, 14 + 4 * mine_crossed)

    zcopies = [
        remote(zbuf.at[zh], zbuf.at[zh], zs.at[d - 1], zr.at[d - 1], device(zh_=rem(zh + d, 4))) for d in range(1, 4)
    ]
    for c in zcopies:
        c.start()
    lcopies = [
        remote(
            lall.at[zl, y], lall.at[zl, y], ls.at[k - 1], lr.at[k - 1],
            device(y_=rem(y + k // 2, 4), zl_=rem(zl + k % 2, 2)),
        )
        for k in range(1, 8)
    ]
    for c in lcopies:
        c.start()

    wf_ref[...] = wm_ref[...].astype(F32)
    for e in range(32):
        wec_ref[32 * e : 32 * e + 32, :] = wf_ref[pl.ds(e, 32, stride=32), :].astype(BF)
    wt_ref[...] = wec_ref[...].astype(F32).T.astype(BF)
    dt_ref[...] = delta_ref[...].astype(F32).reshape(1024, 128).T
    perm2_ref[...] = ones_where(
        ((rows >> 7) == ((cols >> 4) & 3)) & (((rows >> 4) & 7) == (cols >> 6)) & ((rows & 15) == (cols & 15))
    ).astype(BF)

    jb = 2 * rem(x, 2) + core
    ycopies = []
    for d in range(4):
        if d:
            zcopies[d - 1].wait_recv()
        t = rem(zh + 4 - d, 4)
        c = remote(zbuf.at[t], rall.at[jb, zl, y], ys.at[d], yr.at[y], device(x_=tx, y_=t, zl_=tzl))
        ycopies.append(c)
        stays = jnp.logical_and(mine_crossed == 0, t == y)

        @pl.when(stays)
        def _(t=t):
            pltpu.make_async_copy(zbuf.at[t], rall.at[jb, zl, y], yr.at[y]).start()

        @pl.when(jnp.logical_not(stays))
        def _(c=c):
            c.start()

    def group(x_, core_):
        gx_, gzl_ = twin(x_)
        return rall.at[2 * rem(gx_, 2) + core_, gzl_]

    own = group(x, core)
    for t in range(4):
        pltpu.make_async_copy(own.at[t], own.at[t], yr.at[t]).wait()
    xcopies = [
        remote(own, own, xs.at[d - 1], xr.at[d - 1], device(x_=rem(x + d, 4))) for d in range(1, 4)
    ]
    for c in xcopies:
        c.start()
    ccopies = []
    for d in range(4):
        g = group(rem(x + 4 - d, 4), core)
        if d:
            xcopies[d - 1].wait_recv()
        c = remote(g, g, cs.at[d], cr.at[d], device(core_=other))
        c.start()
        ccopies.append(c)
    for c in lcopies:
        c.wait_recv()
    left_ref_blocks = [lall[b // 4, b % 4] for b in range(8)]
    for b in range(8):
        for l in range(4):
            for h in range(2):
                left_ref[32 * b + 16 * h : 32 * b + 16 * h + 16, 128 * l : 128 * l + 128] = left_ref_blocks[b][2 * l + h]
    for c in ccopies:
        c.wait_recv()

    mi = jnp.concatenate([lall[b // 4, b % 4, 8] for b in range(8)], axis=1)
    mj = jnp.concatenate(
        [jnp.concatenate([rall[g, b // 4, b % 4, 8] for b in range(8)], axis=1) for g in range(4)], axis=0
    )
    count = dot(mi, mj, 1, 1)
    lane = iota((16, 1024), 1)
    spread = dot(count.astype(BF), ones_where(iota((64, 1024), 0) == (iota((64, 1024), 1) & 63)).astype(BF))
    denom = jnp.sum(jnp.where((lane >> 6) == iota((16, 1024), 0), spread, 0.0), axis=0, keepdims=True) + 0.001
    scaled = (dt_ref[...] / denom).astype(BF)

    for l in range(4):
        packed = jnp.concatenate([rall[g, :, :, 2 * l : 2 * l + 2].reshape(256, 128) for g in range(4)], axis=1)
        right_ref[:, 512 * l : 512 * l + 512] = dot(packed, perm2_ref[...]).astype(BF)

    gcopies = []
    for l in range(4):
        tile_ref[...] = dot(wec_ref[256 * l : 256 * l + 256, :], scaled)

        def spread_pair(p, carry, l=l):
            lanes = pl.ds(pl.multiple_of(p * 128, 128), 128)
            for t in range(4):
                a, b = swap_halves(tile_ref[64 * t : 64 * t + 32, lanes], tile_ref[64 * t + 32 : 64 * t + 64, lanes])
                place = slice(512 * l + 128 * t, 512 * l + 128 * t + 128)
                d_ref[pl.ds(pl.multiple_of(p * 64, 64), 32), place] = a.astype(BF)
                d_ref[pl.ds(pl.multiple_of(p * 64 + 32, 32), 32), place] = b.astype(BF)
            return carry

        lax.fori_loop(0, 8, spread_pair, 0)
        part = dot(left_ref[...], d_ref[:, 512 * l : 512 * l + 512]).astype(BF)
        part = dot(part, perm2_ref[...], 1, 1).astype(BF)
        for g in range(4):
            gsend[l, g % 2, g // 2] = part[:, 128 * g : 128 * g + 128].reshape(2, 4, 2, 16, 128)
        c = remote(gsend.at[l, other], gcore.at[l], bcs.at[l], bcr.at[l], device(core_=other))
        c.start()
        gcopies.append(c)

    part = dot(right_ref[...], d_ref[...], 1, 1)
    lsend[...] = part.astype(BF).reshape(8, 32, 512)
    blcopies = []
    for k in range(1, 8):
        y_, zl_ = rem(y + k // 2, 4), rem(zl + k % 2, 2)
        c = remote(lsend.at[zl_ * 4 + y_], lrecv.at[k - 1], bls.at[k - 1], blr.at[k - 1], device(y_=y_, zl_=zl_))
        c.start()
        blcopies.append(c)

    bxcopies = []
    for l in range(4):
        gcopies[l].wait_recv()
        hsend[l] = (gsend[l, core].astype(F32) + gcore[l].astype(F32)).astype(BF)
        for d in range(1, 4):
            x_ = rem(x + d, 4)
            gx_, gzl_ = twin(x_)
            c = remote(
                hsend.at[l, rem(gx_, 2), gzl_], gx.at[l, d - 1], bxs.at[l, d - 1], bxr.at[l, d - 1], device(x_=x_)
            )
            c.start()
            bxcopies.append(c)

    def pair_part(l):
        o = dot(left_ref[...], right_ref[:, 512 * l : 512 * l + 512], 0, 0)
        for t in range(4):
            for p in range(8):
                a, b = swap_halves(
                    o[64 * p : 64 * p + 32, 128 * t : 128 * t + 128],
                    o[64 * p + 32 : 64 * p + 64, 128 * t : 128 * t + 128],
                )
                tile_ref[64 * t : 64 * t + 32, 128 * p : 128 * p + 128] = a
                tile_ref[64 * t + 32 : 64 * t + 64, 128 * p : 128 * p + 128] = b
        term = dot(wt_ref[:, 256 * l : 256 * l + 256], tile_ref[...].astype(BF))
        if l == 0:
            pt_ref[...] = term
        else:
            pt_ref[...] += term

    for l in range(4):
        pair_part(l)

    for l in range(4):
        for d in range(3):
            bxcopies[3 * l + d].wait_recv()
        total = hsend[l, rem(tx, 2), tzl].astype(F32)
        for d in range(3):
            total = total + gx[l, d].astype(F32)
        ksend[:, 2 * l : 2 * l + 2] = total.astype(BF)

    bycopies = []
    for d in range(4):
        t = rem(y + d, 4)
        c = remote(ksend.at[t], gy.at[y], bys.at[d], byr.at[y], device(x_=tx, y_=t, zl_=tzl))
        bycopies.append(c)
        if d == 0:

            @pl.when(mine_crossed == 0)
            def _():
                pltpu.make_async_copy(ksend.at[y], gy.at[y], byr.at[y]).start()

            @pl.when(mine_crossed == 1)
            def _(c=c):
                c.start()
        else:
            c.start()

    pair_ref[...] = (pt_ref[...] / denom).T.astype(BF).reshape(16, 64, 128)

    for c in blcopies:
        c.wait_recv()
    dl = lsend[zl * 4 + y].astype(F32)
    for k in range(7):
        dl = dl + lrecv[k].astype(F32)
    dl = dl * mask1_ref[...]

    for t in range(4):
        pltpu.make_async_copy(gy.at[t], gy.at[t], byr.at[t]).wait()
    bzcopies = []
    for d in range(1, 4):
        t = rem(zh + d, 4)
        c = remote(gy.at[t], gz.at[d - 1], bzs.at[d - 1], bzr.at[d - 1], device(zh_=t))
        c.start()
        bzcopies.append(c)
    for c in bzcopies:
        c.wait_recv()
    total = gy[zh].astype(F32)
    for d in range(3):
        total = total + gz[d].astype(F32)
    dr = jnp.concatenate(
        [jnp.concatenate([total[2 * l], total[2 * l + 1]], axis=0) for l in range(4)], axis=1
    ) * mask2_ref[...]
    hi, lo = split(dr)
    dr = dot(hi, perm1_ref[...], 1, 1) + dot(lo, perm1_ref[...], 1, 1)

    rows_i = jnp.concatenate(
        [
            jnp.concatenate([dl[:, 32 * i : 32 * i + 32], dr[:, 32 * i : 32 * i + 32]], axis=1)
            for i in range(16)
        ],
        axis=0,
    )
    hi, lo = split(rows_i)
    w = jnp.concatenate([w1_ref[...], w2_ref[...]], axis=1)
    dn = dot(hi, w, 1, 1) + dot(lo, w, 1, 1)
    for i in range(16):
        for h in range(2):
            dn_ref[h, pl.ds(i, 32, stride=16), :] = dn[32 * i : 32 * i + 32, 128 * h : 128 * h + 128]
    dn = jnp.concatenate([dn_ref[0], dn_ref[1]], axis=1) * gain_ref[...]
    xhat = xhat_ref[...]
    dx = rstd_ref[:, 0:1] * (
        dn - jnp.mean(dn, axis=-1, keepdims=True) - xhat * jnp.mean(dn * xhat, axis=-1, keepdims=True)
    )
    grad_ref[...] = dx.astype(BF).reshape(32, 16, 256)

    for c in zcopies + lcopies + xcopies + ccopies + gcopies + blcopies + bxcopies + bzcopies:
        c.wait_send()
    for d in range(4):
        t = rem(zh + 4 - d, 4)

        @pl.when(jnp.logical_not(jnp.logical_and(mine_crossed == 0, t == y)))
        def _(c=ycopies[d]):
            c.wait_send()

    @pl.when(mine_crossed == 1)
    def _():
        bycopies[0].wait_send()

    for c in bycopies[1:]:
        c.wait_send()


def body(
    homolog_stack,
    presence_flags,
    normalizer_scaling,
    normalizer_offset,
    first_factor_matrix,
    first_factor_offset,
    second_factor_matrix,
    second_factor_offset,
    final_mapping_matrix,
    coupling_delta_cotangent,
):
    dma = pltpu.SemaphoreType.DMA
    vm = pltpu.VMEM
    whole = pl.BlockSpec(memory_space=pltpu.VMEM)
    return tuple(
        pl.pallas_call(
            kernel,
            out_shape=(
                jax.ShapeDtypeStruct((16, 64, 128), BF),
                jax.ShapeDtypeStruct((32, 16, 256), BF),
            ),
            in_specs=[whole] * 10,
            out_specs=(whole, whole),
            scratch_shapes=[
                vm((512, 256), F32),
                vm((512, 128), F32),
                vm((512, 128), F32),
                vm((1024, 128), F32),
                vm((1024, 128), BF),
                vm((128, 1024), BF),
                vm((128, 1024), F32),
                vm((32, 512), F32),
                vm((32, 512), F32),
                vm((512, 512), BF),
                vm((512, 512), BF),
                vm((4, 9, 16, 128), BF),
                vm((2, 4, 9, 16, 128), BF),
                vm((4, 2, 4, 9, 16, 128), BF),
                vm((256, 512), BF),
                vm((256, 2048), BF),
                vm((256, 1024), F32),
                vm((512, 2048), BF),
                vm((128, 1024), F32),
                vm((4, 2, 2, 2, 4, 2, 16, 128), BF),
                vm((4, 2, 2, 4, 2, 16, 128), BF),
                vm((4, 2, 2, 4, 2, 16, 128), BF),
                vm((4, 3, 4, 2, 16, 128), BF),
                vm((4, 8, 16, 128), BF),
                vm((4, 8, 16, 128), BF),
                vm((3, 8, 16, 128), BF),
                vm((8, 32, 512), BF),
                vm((7, 32, 512), BF),
                vm((2, 512, 128), F32),
                dma((3,)), dma((3,)),
                dma((4,)), dma((4,)),
                dma((3,)), dma((3,)),
                dma((4,)), dma((4,)),
                dma((7,)), dma((7,)),
                dma((3,)), dma((3,)),
                dma((4,)), dma((4,)),
                dma((4, 3)), dma((4, 3)),
                dma((4,)), dma((4,)),
                dma((7,)), dma((7,)),
            ],
            compiler_params=pltpu.CompilerParams(
                collective_id=0, has_side_effects=True, vmem_limit_bytes=48 * 1024 * 1024
            ),
        )(
            homolog_stack,
            presence_flags,
            normalizer_scaling.reshape(1, 256),
            normalizer_offset.reshape(1, 256),
            first_factor_matrix,
            first_factor_offset.reshape(1, 32),
            second_factor_matrix,
            second_factor_offset.reshape(1, 32),
            final_mapping_matrix,
            coupling_delta_cotangent,
        )
    )


def solution(mesh):
    return jax.shard_map(
        body,
        mesh=mesh,
        in_specs=(
            P("seq", "res", None),
            P("seq", "res"),
            P(),
            P(),
            P(),
            P(),
            P(),
            P(),
            P(),
            P("res", "seq", None),
        ),
        out_specs=(P("res", "seq", None), P("seq", "res", None)),
        check_vma=False,
    )
```

time: 315 us -> 68.4 us (0.22)
  the two profiles are of different devices: /device:TPU:32 before, /device:TPU:58 now
where the time goes in v1:
time: 68.4 us; the launch traced here: 68.1 us
  Pallas kernels  61 us (89%)
  local copies, waits for them, and re-layouts  6.45 us (9%)
    pallas_call x1, Pallas kernels, body(): pl.pallas_call(kernel, out_shape=(jax.ShapeDtypeStruct((16, 64, 128), BF)...  61 us
    unnamed x23, local copies, waits for them, and re-layouts  6.45 us

profile of v1, /device:TPU:58, one launch (start us, length us, event | category | flops | bytes accessed | tf_op | source)
XLA Modules:
  0.0 68.1 jit_solution(5141853066744220901)
XLA Ops:
  0.6 0.0 copy-start.7
  0.6 0.8 %copy.12.flag_ref = s32[32,16]{1,0:T(8,128)S(1)} copy(s32[32,16]{0,1:T(8,128)} %param.11) | data formatting | bytes 4096 | tf_op args[1]
  1.4 0.0 copy-done.7
  1.4 0.0 copy-start.8
  1.4 0.1 copy.13.w1_ref
  1.5 0.6 copy-done.8
  2.1 0.0 copy-start.3
  2.1 0.0 copy-start.4
  2.1 0.0 copy-start.5
  2.1 0.0 copy-start.6
  2.1 0.1 copy.14.w2_ref
  2.3 0.5 copy-done.3
  2.8 0.0 copy-done.4
  2.8 0.0 copy-done.5
  2.8 0.0 copy-done.6
  2.8 0.0 copy-start
  2.8 0.9 %copy-done = bf16[32,16,256]{2,1,0:T(8,128)(2,1)S(1)} copy-done((bf16[32,16,256]{2,1,0:T(8,128)(2,1)S(1)}, bf16[32,16,256]{2,1,0:T(8,128)(2,1)}, u32[]{:S(2)}) %copy-start) | copy-done | bytes 262168
  3.8 0.0 copy-start.1
  3.8 0.9 %copy-done.1 = bf16[1024,128]{1,0:T(8,128)(2,1)S(1)} copy-done((bf16[1024,128]{1,0:T(8,128)(2,1)S(1)}, bf16[1024,128]{1,0:T(8,128)(2,1)}, u32[]{:S(2)}) %copy-start.1) | copy-done | bytes 262168
  4.7 0.0 copy-start.2
  4.7 0.9 %copy-done.2 = bf16[16,64,128]{2,1,0:T(8,128)(2,1)S(1)} copy-done((bf16[16,64,128]{2,1,0:T(8,128)(2,1)S(1)}, bf16[16,64,128]{2,1,0:T(8,128)(2,1)}, u32[]{:S(2)}) %copy-start.2) | copy-done | bytes 262168
  5.7 61.0 %shard_map.113 = (bf16[16,64,128]{2,1,0:T(8,128)(2,1)S(1)}, bf16[32,16,256]{2,1,0:T(8,128)(2,1)S(1)}) custom-call(bf16[32,16,256]{2,1,0:T(8,128)(2,1)S(1)} %copy-done, s32[32,16]{1,0:T(8,128)S(1)} %copy.12.flag_ref, f32[1,256]{1,0:T(1,128)S(1)} %bitcast.4, f32[1,256]{1,0:T(1,128)S(1)} %bitcast.5, bf16[256,32]{1,0:T(8,128)(2,1)S(1)} %copy.13.w1_ref, ...), custom_call_target="tpu_custom_call" | custom-call | tf_op jit(solution)/shard_map/pallas_call | solution.py:384
  66.7 0.7 %copy.17 = bf16[16,64,128]{2,1,0:T(8,128)(2,1)} copy(bf16[16,64,128]{2,1,0:T(8,128)(2,1)S(1)} %get-tuple-element.4) | data formatting | bytes 524288
  67.4 0.7 %copy.18 = bf16[32,16,256]{2,1,0:T(8,128)(2,1)} copy(bf16[32,16,256]{2,1,0:T(8,128)(2,1)S(1)} %get-tuple-element.5) | data formatting | bytes 524288
Async XLA Ops:
  0.6 0.8 %copy-start.7 = (bf16[256,32]{0,1:T(8,128)(2,1)S(1)}, bf16[256,32]{0,1:T(8,128)(2,1)}, u32[]{:S(2)}) copy-start(bf16[256,32]{0,1:T(8,128)(2,1)} %param.14) | copy-start | bytes 49156
  1.4 0.7 %copy-start.8 = (bf16[256,32]{0,1:T(8,128)(2,1)S(1)}, bf16[256,32]{0,1:T(8,128)(2,1)}, u32[]{:S(2)}) copy-start(bf16[256,32]{0,1:T(8,128)(2,1)} %param.16) | copy-start | bytes 49156
  2.1 0.7 copy-start.3
  2.1 0.7 %copy-start.4 = (f32[256]{0:T(256)S(1)}, f32[256]{0:T(256)}, u32[]{:S(2)}) copy-start(f32[256]{0:T(256)} %param.13) | copy-start | bytes 3076
  2.1 0.7 %copy-start.5 = (f32[32]{0:T(128)S(1)}, f32[32]{0:T(128)}, u32[]{:S(2)}) copy-start(f32[32]{0:T(128)} %param.15) | copy-start | bytes 388
  2.1 0.7 %copy-start.6 = (f32[32]{0:T(128)S(1)}, f32[32]{0:T(128)}, u32[]{:S(2)}) copy-start(f32[32]{0:T(128)} %param.17) | copy-start | bytes 388
  2.8 0.9 %copy-start = (bf16[32,16,256]{2,1,0:T(8,128)(2,1)S(1)}, bf16[32,16,256]{2,1,0:T(8,128)(2,1)}, u32[]{:S(2)}) copy-start(bf16[32,16,256]{2,1,0:T(8,128)(2,1)} %x_ref.1) | copy-start | bytes 786436
  3.8 0.9 %copy-start.1 = (bf16[1024,128]{1,0:T(8,128)(2,1)S(1)}, bf16[1024,128]{1,0:T(8,128)(2,1)}, u32[]{:S(2)}) copy-start(bf16[1024,128]{1,0:T(8,128)(2,1)} %wm_ref.1) | copy-start | bytes 786436
  4.7 0.9 %copy-start.2 = (bf16[16,64,128]{2,1,0:T(8,128)(2,1)S(1)}, bf16[16,64,128]{2,1,0:T(8,128)(2,1)}, u32[]{:S(2)}) copy-start(bf16[16,64,128]{2,1,0:T(8,128)(2,1)} %delta_ref.1) | copy-start | bytes 786436

commit v2 on v1

v2 whole, which is shorter than its diff:
```python
import jax
import jax.numpy as jnp
from jax import lax
from jax.experimental import pallas as pl
from jax.experimental.pallas import tpu as pltpu
from jax.sharding import PartitionSpec as P

F32 = jnp.float32
BF = jnp.bfloat16
MESH = pl.DeviceIdType.MESH


def dot(a, b, ca=1, cb=0):
    return lax.dot_general(a, b, (((ca,), (cb,)), ((), ())), preferred_element_type=F32)


def rem(a, n):
    return lax.rem(a, jnp.int32(n))


def div(a, n):
    return lax.div(a, jnp.int32(n))


def split(a):
    hi = a.astype(BF)
    return hi, (a - hi.astype(F32)).astype(BF)


def ones_where(condition):
    return jnp.where(condition, 1.0, 0.0)


def iota(shape, dim):
    return lax.broadcasted_iota(jnp.int32, shape, dim)


def swap_halves(a, b):
    low = iota(a.shape, 1) < 64
    return (
        jnp.where(low, a, pltpu.roll(b, 64, 1)),
        jnp.where(low, pltpu.roll(a, 64, 1), b),
    )


NEAR = ((0, 0), (0, 1), (0, 3), (1, 0), (3, 0), (1, 1), (1, 3), (3, 1), (3, 3), (0, 2), (2, 0), (1, 2), (3, 2), (2, 1), (2, 3), (2, 2))


def kernel(
    x_hbm, flag_hbm, gain_hbm, shift_hbm, w1_hbm, b1_hbm, w2_hbm, b2_hbm, wm_hbm, delta_hbm,
    pair_ref, grad_ref,
    x_ref, flag_ref, gain_ref, shift_ref, w1_ref, b1_ref, w2_ref, b2_ref, wm_ref, delta_ref, in_sem,
    xhat_ref, rstd_ref, proj_ref, wf_ref, wec_ref, wt_ref, dt_ref, mask1_ref, mask2_ref, perm1_ref, perm2_ref,
    wire, zbuf, lall, rall, left_ref, right_ref, tile_ref, d_ref, rec_ref, pt_ref,
    gsend, gcore, hsend, gx, ksend, gz, lsend, lrecv, dn_ref,
    zs, zr, bs, br, cs, cr, ls, lr,
    gcs, gcr, gbs, gbr, gzs, gzr, gls, glr,
):
    inputs = [
        pltpu.make_async_copy(a, b, in_sem.at[n])
        for n, (a, b) in enumerate(
            zip(
                (x_hbm, flag_hbm, gain_hbm, shift_hbm, w1_hbm, b1_hbm, w2_hbm, b2_hbm, wm_hbm, delta_hbm),
                (x_ref, flag_ref, gain_ref, shift_ref, w1_ref, b1_ref, w2_ref, b2_ref, wm_ref, delta_ref),
            )
        )
    ]
    for c in inputs:
        c.start()

    q = lax.axis_index("seq")
    r = lax.axis_index("res")
    y, zl = div(q, 2), rem(q, 2)
    zh, x, core = div(r, 8), rem(div(r, 2), 4), rem(r, 2)
    other = 1 - core

    def device(x_=x, y_=y, zh_=zh, zl_=zl, core_=core):
        return {"seq": y_ * 2 + zl_, "res": zh_ * 8 + x_ * 2 + core_}

    def twin(x_):
        m = rem(div(x_, 2) + zl, 2)
        return x_ + m * (3 - 2 * x_), rem(zl + m, 2)

    crossed = rem(div(x, 2) + zl, 2)
    tx, tzl = twin(x)

    def remote(src, dst, send, recv, where):
        return pltpu.make_async_remote_copy(
            src_ref=src, dst_ref=dst, send_sem=send, recv_sem=recv, device_id=where, device_id_type=MESH
        )

    def landed(ref, sem):
        pltpu.make_async_copy(ref, ref, sem).wait()

    barrier = pltpu.get_barrier_semaphore()

    def greet(where):
        pl.semaphore_signal(barrier, inc=1, device_id=where, device_id_type=MESH)

    for d in (2, 1, 3):
        greet(device(x_=tx, zl_=tzl, zh_=rem(zh + d, 4)))

    @pl.when(crossed == 1)
    def _():
        greet(device(x_=tx, zl_=tzl))

    for dx, dy in NEAR[1:]:
        greet(device(x_=rem(x + dx, 4), y_=rem(y + dy, 4)))
    for dy in range(4):
        greet(device(y_=rem(y + dy, 4), zl_=1 - zl))
    greet(device(core_=other))

    rows, cols = iota((512, 512), 0), iota((512, 512), 1)
    perm1 = ones_where(((rows >> 5) == (cols & 15)) & ((rows & 31) == (cols >> 4))).astype(BF)
    perm1_ref[...] = perm1
    for c in inputs[:8]:
        c.wait()
    xv = x_ref[...].astype(F32).reshape(512, 256)
    centred = xv - jnp.mean(xv, axis=-1, keepdims=True)
    rstd = lax.rsqrt(jnp.mean(centred * centred, axis=-1, keepdims=True) + 1e-5)
    xhat = centred * rstd
    xhat_ref[...] = xhat
    rstd_ref[...] = jnp.broadcast_to(rstd, (512, 128))
    hi, lo = split(xhat * gain_ref[...] + shift_ref[...])
    w = jnp.concatenate([w1_ref[...], w2_ref[...]], axis=0)
    bias = jnp.concatenate([b1_ref[...], b2_ref[...]], axis=1)
    proj_ref[:, 0:64] = dot(hi, w, 1, 1) + dot(lo, w, 1, 1) + bias

    flags_t = flag_ref[...].astype(F32).astype(BF)
    mask1 = dot(flags_t, ones_where(iota((16, 512), 0) == (iota((16, 512), 1) >> 5)).astype(BF), 0, 0)
    mask2 = dot(flags_t, ones_where(iota((16, 512), 0) == (iota((16, 512), 1) & 15)).astype(BF), 0, 0)
    mask1_ref[...] = mask1
    mask2_ref[...] = mask2
    flags_t = jnp.concatenate([flags_t, jnp.zeros((16, 96), BF)], axis=1)
    parts = [proj_ref[pl.ds(i, 32, stride=16), :] for i in range(16)]
    lw = (jnp.concatenate([p[:, 0:32] for p in parts], axis=1) * mask1).astype(BF)
    rw = jnp.concatenate([p[:, 32:64] for p in parts], axis=1).astype(BF)
    rw = (dot(rw, perm1) * mask2).astype(BF)
    for l in range(4):
        for h in range(2):
            lall[zl, y, 2 * l + h] = lw[16 * h : 16 * h + 16, 128 * l : 128 * l + 128]
            wire[2 * l + h] = rw[16 * h : 16 * h + 16, 128 * l : 128 * l + 128]
    lall[zl, y, 8] = flags_t
    wire[8] = flags_t

    pl.semaphore_wait(barrier, 23 + crossed)

    zcopies = {}
    for d in (2, 1, 3, 0):
        zcopies[d] = remote(
            wire, zbuf.at[zh], zs.at[d], zr.at[d], device(x_=tx, zl_=tzl, zh_=rem(zh + d, 4))
        )
    for d in (2, 1, 3):
        zcopies[d].start()

    @pl.when(crossed == 1)
    def _():
        zcopies[0].start()

    @pl.when(crossed == 0)
    def _():
        pltpu.make_async_copy(wire, zbuf.at[zh], zr.at[0]).start()

    lcopies = [
        remote(
            lall.at[zl, y], lall.at[zl, y], ls.at[k - 1], lr.at[k - 1],
            device(y_=rem(y + k // 2, 4), zl_=rem(zl + k % 2, 2)),
        )
        for k in range(1, 8)
    ]

    def send_left():
        for c in lcopies:
            c.start()

    jb = 2 * rem(tx, 2) + core
    bcopies = {}

    def spread_out(d):
        t = rem(zh + 4 - d, 4)
        landed(zbuf.at[t], zr.at[d])
        for dx in (2, 1, 3, 0):
            c = remote(
                zbuf.at[t], rall.at[jb, tzl, y], bs.at[d, dx], br.at[x, y], device(x_=rem(x + dx, 4), y_=t)
            )
            bcopies[d, dx] = c
            if dx:
                c.start()
            else:

                @pl.when(t == y)
                def _():
                    pltpu.make_async_copy(zbuf.at[t], rall.at[jb, tzl, y], br.at[x, y]).start()

                @pl.when(t != y)
                def _():
                    c.start()

    spread_out(0)
    send_left()
    for c in inputs[8:]:
        c.wait()
    wf_ref[...] = wm_ref[...].astype(F32)
    for e in range(32):
        wec_ref[32 * e : 32 * e + 32, :] = wf_ref[pl.ds(e, 32, stride=32), :].astype(BF)
    dt_ref[...] = delta_ref[...].astype(F32).reshape(1024, 128).T.astype(BF)
    spread_out(1)
    spread_out(3)
    perm2_ref[...] = ones_where(
        ((rows >> 7) == ((cols >> 4) & 3)) & (((rows >> 4) & 7) == (cols >> 6)) & ((rows & 15) == (cols & 15))
    ).astype(BF)
    wt_ref[...] = wec_ref[...].astype(F32).T.astype(BF)
    spread_out(2)

    for l in range(4):
        tile_ref[...] = dot(wec_ref[256 * l : 256 * l + 256, :], dt_ref[...])

        def spread_pair(p, carry, l=l):
            lanes = pl.ds(pl.multiple_of(p * 128, 128), 128)
            for t in range(4):
                a, b = swap_halves(tile_ref[64 * t : 64 * t + 32, lanes], tile_ref[64 * t + 32 : 64 * t + 64, lanes])
                place = slice(512 * l + 128 * t, 512 * l + 128 * t + 128)
                d_ref[pl.ds(pl.multiple_of(p * 64, 64), 32), place] = a.astype(BF)
                d_ref[pl.ds(pl.multiple_of(p * 64 + 32, 32), 32), place] = b.astype(BF)
            return carry

        lax.fori_loop(0, 8, spread_pair, 0)

    ccopies = []
    for n, (dx, dy) in enumerate(NEAR):
        xs, ys = rem(x + dx, 4), rem(y + dy, 4)
        gx_, gzl_ = twin(xs)
        block = rall.at[2 * rem(gx_, 2) + core, gzl_, ys]
        landed(block, br.at[xs, ys])
        c = remote(block, block, cs.at[n], cr.at[n], device(core_=other))
        c.start()
        ccopies.append(c)
    for c in lcopies:
        c.wait_recv()
    for b in range(8):
        for l in range(4):
            for h in range(2):
                left_ref[32 * b + 16 * h : 32 * b + 16 * h + 16, 128 * l : 128 * l + 128] = lall[b // 4, b % 4, 2 * l + h]
    for c in ccopies:
        c.wait_recv()

    mi = jnp.concatenate([lall[b // 4, b % 4, 8] for b in range(8)], axis=1)
    mj = jnp.concatenate(
        [jnp.concatenate([rall[g, b // 4, b % 4, 8] for b in range(8)], axis=1) for g in range(4)], axis=0
    )
    count = dot(mi, mj, 1, 1)
    count = dot(count.astype(BF), ones_where(iota((64, 128), 0) == (iota((64, 128), 1) & 63)).astype(BF))
    rec_ref[...] = 1.0 / (count + 0.001)

    def scale(i, carry):
        here = pl.ds(pl.multiple_of(i * 32, 32), 32)
        factor = jnp.broadcast_to(rec_ref[pl.ds(i, 1), :], (32, 128))
        for t in range(16):
            lanes = slice(128 * t, 128 * t + 128)
            d_ref[here, lanes] = (d_ref[here, lanes].astype(F32) * factor).astype(BF)
        return carry

    lax.fori_loop(0, 16, scale, 0)

    gcopies = []
    for n in range(2):
        half = rem(tzl + 1 + n, 2)
        part = dot(left_ref[pl.ds(pl.multiple_of(half * 128, 128), 128), :], d_ref[...]).astype(BF)
        for l in range(4):
            piece = dot(part[:, 512 * l : 512 * l + 512], perm2_ref[...], 1, 1).astype(BF)
            for g in range(4):
                gsend[half, g % 2, g // 2, :, 2 * l : 2 * l + 2] = piece[:, 128 * g : 128 * g + 128].reshape(4, 2, 16, 128)
        c = remote(gsend.at[half, other], gcore.at[half], gcs.at[n], gcr.at[n], device(core_=other))
        c.start()
        gcopies.append(c)

    gbcopies = []
    for n in range(2):
        half = rem(tzl + 1 + n, 2)
        gcopies[n].wait_recv()
        hsend[half] = (gsend[half, core].astype(F32) + gcore[half].astype(F32)).astype(BF)
        for m in range(2):
            x_ = 2 * rem(div(x, 2) + 1 + n, 2) + rem(x + 1 + m, 2)
            hx, _ = twin(x_)
            for dy in (2, 1, 3, 0):
                y_ = rem(y + dy, 4)
                src = hsend.at[half, rem(hx, 2), y_]
                if n == 1 and m == 1 and dy == 0:
                    pltpu.make_async_copy(src, gx.at[x, y], gbr.at[x, y]).start()
                else:
                    c = remote(src, gx.at[x, y], gbs.at[n, m, dy], gbr.at[x, y], device(x_=x_, y_=y_))
                    c.start()
                    gbcopies.append(c)

    for l in range(4):
        packed = jnp.concatenate([rall[g, :, :, 2 * l : 2 * l + 2].reshape(256, 128) for g in range(4)], axis=1)
        right_ref[:, 512 * l : 512 * l + 512] = dot(packed, perm2_ref[...]).astype(BF)
    part = dot(right_ref[...], d_ref[...], 1, 1)
    lsend[...] = part.astype(BF).reshape(8, 32, 512)
    glcopies = []
    for k in (4, 5, 2, 3, 6, 7, 1):
        y_, zl_ = rem(y + k // 2, 4), rem(zl + k % 2, 2)
        c = remote(lsend.at[zl_ * 4 + y_], lrecv.at[k - 1], gls.at[k - 1], glr.at[k - 1], device(y_=y_, zl_=zl_))
        c.start()
        glcopies.append(c)

    def pair_part(l):
        o = dot(left_ref[...], right_ref[:, 512 * l : 512 * l + 512], 0, 0)
        for t in range(4):
            for p in range(8):
                a, b = swap_halves(
                    o[64 * p : 64 * p + 32, 128 * t : 128 * t + 128],
                    o[64 * p + 32 : 64 * p + 64, 128 * t : 128 * t + 128],
                )
                tile_ref[64 * t : 64 * t + 32, 128 * p : 128 * p + 128] = a
                tile_ref[64 * t + 32 : 64 * t + 64, 128 * p : 128 * p + 128] = b
        term = dot(wt_ref[:, 256 * l : 256 * l + 256], tile_ref[...].astype(BF))
        if l == 0:
            pt_ref[...] = term
        else:
            pt_ref[...] += term

    pair_part(0)
    pair_part(1)

    gzcopies = {}
    for d in (2, 1, 3, 0):
        t = rem(zh + d, 4)
        for s in range(4):
            landed(gx.at[s, t], gbr.at[s, t])
        total = gx[0, t].astype(F32) + gx[1, t].astype(F32) + gx[2, t].astype(F32) + gx[3, t].astype(F32)
        ksend[t] = total.astype(BF)
        c = remote(ksend.at[t], gz.at[zh], gzs.at[d], gzr.at[d], device(x_=tx, zl_=tzl, zh_=t))
        gzcopies[d] = c
        if d:
            c.start()
        else:

            @pl.when(crossed == 1)
            def _():
                c.start()

            @pl.when(crossed == 0)
            def _():
                pltpu.make_async_copy(ksend.at[zh], gz.at[zh], gzr.at[0]).start()

    pair_part(2)
    pair_part(3)
    factor = jnp.concatenate(
        [
            jnp.where(iota((1, 128), 1) < 64, rec_ref[2 * p : 2 * p + 1, :], rec_ref[2 * p + 1 : 2 * p + 2, :])
            for p in range(8)
        ],
        axis=1,
    )
    pair_ref[...] = (pt_ref[...] * factor).T.astype(BF).reshape(16, 64, 128)

    for c in glcopies:
        c.wait_recv()
    dl = lsend[zl * 4 + y].astype(F32)
    for k in range(7):
        dl = dl + lrecv[k].astype(F32)
    dl = dl * mask1_ref[...]

    for d in (0, 1, 3, 2):
        t = rem(zh + 4 - d, 4)
        landed(gz.at[t], gzr.at[d])
    total = gz[0].astype(F32) + gz[1].astype(F32) + gz[2].astype(F32) + gz[3].astype(F32)
    dr = jnp.concatenate(
        [jnp.concatenate([total[2 * l], total[2 * l + 1]], axis=0) for l in range(4)], axis=1
    ) * mask2_ref[...]
    hi, lo = split(dr)
    dr = dot(hi, perm1_ref[...], 1, 1) + dot(lo, perm1_ref[...], 1, 1)

    rows_i = jnp.concatenate(
        [
            jnp.concatenate([dl[:, 32 * i : 32 * i + 32], dr[:, 32 * i : 32 * i + 32]], axis=1)
            for i in range(16)
        ],
        axis=0,
    )
    hi, lo = split(rows_i)
    dn = dot(hi, w) + dot(lo, w)
    for i in range(16):
        for h in range(2):
            dn_ref[h, pl.ds(i, 32, stride=16), :] = dn[32 * i : 32 * i + 32, 128 * h : 128 * h + 128]
    dn = jnp.concatenate([dn_ref[0], dn_ref[1]], axis=1) * gain_ref[...]
    xhat = xhat_ref[...]
    dx = rstd_ref[:, 0:1] * (
        dn - jnp.mean(dn, axis=-1, keepdims=True) - xhat * jnp.mean(dn * xhat, axis=-1, keepdims=True)
    )
    grad_ref[...] = dx.astype(BF).reshape(32, 16, 256)

    for c in lcopies + ccopies + gcopies + glcopies + gbcopies:
        c.wait_send()
    for d in (1, 2, 3):
        zcopies[d].wait_send()
        gzcopies[d].wait_send()

    @pl.when(crossed == 1)
    def _():
        zcopies[0].wait_send()
        gzcopies[0].wait_send()

    for d in range(4):
        for dx in (1, 2, 3):
            bcopies[d, dx].wait_send()

        @pl.when(rem(zh + 4 - d, 4) != y)
        def _():
            bcopies[d, 0].wait_send()


def body(
    homolog_stack,
    presence_flags,
    normalizer_scaling,
    normalizer_offset,
    first_factor_matrix,
    first_factor_offset,
    second_factor_matrix,
    second_factor_offset,
    final_mapping_matrix,
    coupling_delta_cotangent,
):
    dma = pltpu.SemaphoreType.DMA
    vm = pltpu.VMEM
    whole = pl.BlockSpec(memory_space=pltpu.VMEM)
    far = pl.BlockSpec(memory_space=pltpu.HBM)
    return tuple(
        pl.pallas_call(
            kernel,
            out_shape=(
                jax.ShapeDtypeStruct((16, 64, 128), BF),
                jax.ShapeDtypeStruct((32, 16, 256), BF),
            ),
            in_specs=[far] * 10,
            out_specs=(whole, whole),
            scratch_shapes=[
                vm((32, 16, 256), BF),
                vm((16, 32), jnp.int32),
                vm((1, 256), F32),
                vm((1, 256), F32),
                vm((32, 256), BF),
                vm((1, 32), F32),
                vm((32, 256), BF),
                vm((1, 32), F32),
                vm((1024, 128), BF),
                vm((16, 64, 128), BF),
                dma((10,)),
                vm((512, 256), F32),
                vm((512, 128), F32),
                vm((512, 128), F32),
                vm((1024, 128), F32),
                vm((1024, 128), BF),
                vm((128, 1024), BF),
                vm((128, 1024), BF),
                vm((32, 512), F32),
                vm((32, 512), F32),
                vm((512, 512), BF),
                vm((512, 512), BF),
                vm((9, 16, 128), BF),
                vm((4, 9, 16, 128), BF),
                vm((2, 4, 9, 16, 128), BF),
                vm((4, 2, 4, 9, 16, 128), BF),
                vm((256, 512), BF),
                vm((256, 2048), BF),
                vm((256, 1024), F32),
                vm((512, 2048), BF),
                vm((16, 128), F32),
                vm((128, 1024), F32),
                vm((2, 2, 2, 4, 8, 16, 128), BF),
                vm((2, 2, 4, 8, 16, 128), BF),
                vm((2, 2, 4, 8, 16, 128), BF),
                vm((4, 4, 8, 16, 128), BF),
                vm((4, 8, 16, 128), BF),
                vm((4, 8, 16, 128), BF),
                vm((8, 32, 512), BF),
                vm((7, 32, 512), BF),
                vm((2, 512, 128), F32),
                dma((4,)), dma((4,)),
                dma((4, 4)), dma((4, 4)),
                dma((16,)), dma((16,)),
                dma((7,)), dma((7,)),
                dma((2,)), dma((2,)),
                dma((2, 2, 4)), dma((4, 4)),
                dma((4,)), dma((4,)),
                dma((7,)), dma((7,)),
            ],
            compiler_params=pltpu.CompilerParams(
                collective_id=0, has_side_effects=True, vmem_limit_bytes=63 * 1024 * 1024
            ),
        )(
            homolog_stack,
            presence_flags.T,
            normalizer_scaling.reshape(1, 256),
            normalizer_offset.reshape(1, 256),
            first_factor_matrix.T,
            first_factor_offset.reshape(1, 32),
            second_factor_matrix.T,
            second_factor_offset.reshape(1, 32),
            final_mapping_matrix,
            coupling_delta_cotangent,
        )
    )


def solution(mesh):
    return jax.shard_map(
        body,
        mesh=mesh,
        in_specs=(
            P("seq", "res", None),
            P("seq", "res"),
            P(),
            P(),
            P(),
            P(),
            P(),
            P(),
            P(),
            P("res", "seq", None),
        ),
        out_specs=(P("res", "seq", None), P("seq", "res", None)),
        check_vma=False,
    )
```

time: 68.4 us -> 52.2 us (0.76)
  the two profiles are of different devices: /device:TPU:58 before, /device:TPU:32 now
where the time goes in v2:
time: 52.2 us; the launch traced here: 51.9 us
  Pallas kernels  48.9 us (94%)
  local copies, waits for them, and re-layouts  2.42 us (5%)
  between operations  0.65 us (1%)
    pallas_call x1, Pallas kernels, body(): pl.pallas_call(kernel, out_shape=(jax.ShapeDtypeStruct((16, 64, 128), BF)...  48.9 us
    unnamed x4, local copies, waits for them, and re-layouts  2.42 us

profile of v2, /device:TPU:32, one launch (start us, length us, event | category | flops | bytes accessed | tf_op | source)
XLA Modules:
  0.0 51.9 jit_solution(302746787343015877)
XLA Ops:
  0.6 48.9 %shard_map.113 = (bf16[16,64,128]{2,1,0:T(8,128)(2,1)}, bf16[32,16,256]{2,1,0:T(8,128)(2,1)}) custom-call(bf16[32,16,256]{2,1,0:T(8,128)(2,1)} %x_hbm.1, s32[16,32]{1,0:T(8,128)} %bitcast.9, f32[1,256]{1,0:T(1,128)} %bitcast.10, f32[1,256]{1,0:T(1,128)} %bitcast.11, bf16[32,256]{1,0:T(8,128)(2,1)} %bitcast.7, f32[1,32]{1,0:T(1,128)} %bitcast.12, ...), custom_call_target="tpu_custom_call" | custom-call | tf_op jit(solution)/shard_map/pallas_call | solution.py:431
  49.5 0.0 copy-start
  49.5 1.7 %copy.14 = bf16[16,64,128]{2,1,0:T(8,128)(2,1)} copy(bf16[16,64,128]{2,1,0:T(8,128)(2,1)} %get-tuple-element.4) | data formatting | bytes 524288
  51.2 0.0 copy-done
  51.2 0.7 %copy.15 = bf16[32,16,256]{2,1,0:T(8,128)(2,1)} copy(bf16[32,16,256]{2,1,0:T(8,128)(2,1)S(1)} %copy-done) | data formatting | bytes 524288
Async XLA Ops:
  49.5 1.7 %copy-start = (bf16[32,16,256]{2,1,0:T(8,128)(2,1)S(1)}, bf16[32,16,256]{2,1,0:T(8,128)(2,1)}, u32[]{:S(2)}) copy-start(bf16[32,16,256]{2,1,0:T(8,128)(2,1)} %get-tuple-element.5) | copy-start | bytes 786436

commit v3 on v2

v3 whole, which is shorter than its diff:
```python
import jax
import jax.numpy as jnp
from jax import lax
from jax.experimental import pallas as pl
from jax.experimental.pallas import tpu as pltpu
from jax.sharding import PartitionSpec as P

F32 = jnp.float32
BF = jnp.bfloat16
MESH = pl.DeviceIdType.MESH


def dot(a, b, ca=1, cb=0):
    return lax.dot_general(a, b, (((ca,), (cb,)), ((), ())), preferred_element_type=F32)


def rem(a, n):
    return lax.rem(a, jnp.int32(n))


def div(a, n):
    return lax.div(a, jnp.int32(n))


def split(a):
    hi = a.astype(BF)
    return hi, (a - hi.astype(F32)).astype(BF)


def ones_where(condition):
    return jnp.where(condition, 1.0, 0.0)


def iota(shape, dim):
    return lax.broadcasted_iota(jnp.int32, shape, dim)


def swap_halves(a, b):
    low = iota(a.shape, 1) < 64
    return (
        jnp.where(low, a, pltpu.roll(b, 64, 1)),
        jnp.where(low, pltpu.roll(a, 64, 1), b),
    )


NEAR = ((0, 0), (0, 1), (0, 3), (1, 0), (3, 0), (1, 1), (1, 3), (3, 1), (3, 3), (0, 2), (2, 0), (1, 2), (3, 2), (2, 1), (2, 3), (2, 2))


def kernel(
    x_hbm, flag_hbm, gain_hbm, shift_hbm, w1_hbm, b1_hbm, w2_hbm, b2_hbm, wm_hbm, delta_hbm,
    pair_ref, grad_ref,
    x_ref, flag_ref, gain_ref, shift_ref, w1_ref, b1_ref, w2_ref, b2_ref, wm_ref, delta_ref, in_sem,
    xhat_ref, rstd_ref, proj_ref, wf_ref, wec_ref, wt_ref, dt_ref, mask1_ref, mask2_ref, perm1_ref, perm2_ref,
    fwire, fz, fall, wire, zbuf, lall, rall, left_ref, right_ref, tile_ref, draw_ref, d_ref, rec_ref, pt_ref,
    own_ref, gsend, gcore, hsend, gx, ksend, gz, lsend, lrecv, lsum, lother, dnl_ref, dn_ref,
    fzs, fzr, fbs, fbr, fcs, fcr, zs, zr, bs, br, cs, cr, ls, lr,
    gcs, gcr, gbs, gbr, gzs, gzr, gls, glr,
):
    inputs = [
        pltpu.make_async_copy(a, b, in_sem.at[n])
        for n, (a, b) in enumerate(
            zip(
                (x_hbm, flag_hbm, gain_hbm, shift_hbm, w1_hbm, b1_hbm, w2_hbm, b2_hbm, wm_hbm, delta_hbm),
                (x_ref, flag_ref, gain_ref, shift_ref, w1_ref, b1_ref, w2_ref, b2_ref, wm_ref, delta_ref),
            )
        )
    ]
    for c in inputs:
        c.start()

    q = lax.axis_index("seq")
    r = lax.axis_index("res")
    y, zl = div(q, 2), rem(q, 2)
    zh, x, core = div(r, 8), rem(div(r, 2), 4), rem(r, 2)
    other = 1 - core

    def device(x_=x, y_=y, zh_=zh, zl_=zl, core_=core):
        return {"seq": y_ * 2 + zl_, "res": zh_ * 8 + x_ * 2 + core_}

    def twin(x_):
        m = rem(div(x_, 2) + zl, 2)
        return x_ + m * (3 - 2 * x_), rem(zl + m, 2)

    crossed = rem(div(x, 2) + zl, 2)
    tx, tzl = twin(x)

    def remote(src, dst, send, recv, where):
        return pltpu.make_async_remote_copy(
            src_ref=src, dst_ref=dst, send_sem=send, recv_sem=recv, device_id=where, device_id_type=MESH
        )

    def landed(ref, sem):
        pltpu.make_async_copy(ref, ref, sem).wait()

    barrier = pltpu.get_barrier_semaphore()

    def greet(where):
        pl.semaphore_signal(barrier, inc=1, device_id=where, device_id_type=MESH)

    for d in (2, 1, 3):
        greet(device(x_=tx, zl_=tzl, zh_=rem(zh + d, 4)))

    @pl.when(crossed == 1)
    def _():
        greet(device(x_=tx, zl_=tzl))

    for dx, dy in NEAR[1:]:
        greet(device(x_=rem(x + dx, 4), y_=rem(y + dy, 4)))
    for dy in range(4):
        greet(device(y_=rem(y + dy, 4), zl_=1 - zl))
    greet(device(core_=other))

    inputs[1].wait()
    flags_t = flag_ref[...].astype(F32).astype(BF)
    flags_tile = jnp.concatenate([flags_t, jnp.zeros((16, 96), BF)], axis=1)
    fwire[...] = flags_tile
    lall[zl, y, 8] = flags_tile

    def over_z(src, buf, send, recv):
        copies = {}
        for d in (2, 1, 3, 0):
            copies[d] = remote(src, buf.at[zh], send.at[d], recv.at[d], device(x_=tx, zl_=tzl, zh_=rem(zh + d, 4)))
        for d in (2, 1, 3):
            copies[d].start()

        @pl.when(crossed == 1)
        def _():
            copies[0].start()

        @pl.when(crossed == 0)
        def _():
            pltpu.make_async_copy(src, buf.at[zh], recv.at[0]).start()

        return copies

    def spread_out(d, buf, zrecv, dst, send, recv):
        t = rem(zh + 4 - d, 4)
        landed(buf.at[t], zrecv.at[d])
        place = dst.at[core, rem(tx, 2), tzl, y]
        copies = []
        for dx in (2, 1, 3, 0):
            c = remote(buf.at[t], place, send.at[d, dx], recv.at[x, y], device(x_=rem(x + dx, 4), y_=t))
            copies.append(c)
            if dx:
                c.start()
            else:

                @pl.when(t == y)
                def _():
                    pltpu.make_async_copy(buf.at[t], place, recv.at[x, y]).start()

                @pl.when(t != y)
                def _():
                    c.start()

        return copies

    rows, cols = iota((512, 512), 0), iota((512, 512), 1)
    perm1 = ones_where(((rows >> 5) == (cols & 15)) & ((rows & 31) == (cols >> 4))).astype(BF)
    perm1_ref[...] = perm1
    for n in (0, 2, 3, 4, 5, 6, 7):
        inputs[n].wait()
    xv = x_ref[...].astype(F32).reshape(512, 256)
    centred = xv - jnp.mean(xv, axis=-1, keepdims=True)
    rstd = lax.rsqrt(jnp.mean(centred * centred, axis=-1, keepdims=True) + 1e-5)
    xhat = centred * rstd
    xhat_ref[...] = xhat
    rstd_ref[...] = jnp.broadcast_to(rstd, (512, 128))
    hi, lo = split(xhat * gain_ref[...] + shift_ref[...])
    w = jnp.concatenate([w1_ref[...], w2_ref[...]], axis=0)
    bias = jnp.concatenate([b1_ref[...], b2_ref[...]], axis=1)
    proj_ref[:, 0:64] = dot(hi, w, 1, 1) + dot(lo, w, 1, 1) + bias

    mask1 = dot(flags_t, ones_where(iota((16, 512), 0) == (iota((16, 512), 1) >> 5)).astype(BF), 0, 0)
    mask2 = dot(flags_t, ones_where(iota((16, 512), 0) == (iota((16, 512), 1) & 15)).astype(BF), 0, 0)
    mask1_ref[...] = mask1
    mask2_ref[...] = mask2
    parts = [proj_ref[pl.ds(i, 32, stride=16), :] for i in range(16)]
    lw = (jnp.concatenate([p[:, 0:32] for p in parts], axis=1) * mask1).astype(BF)
    rw = jnp.concatenate([p[:, 32:64] for p in parts], axis=1).astype(BF)
    rw = (dot(rw, perm1) * mask2).astype(BF)
    for l in range(4):
        for h in range(2):
            lall[zl, y, 2 * l + h] = lw[16 * h : 16 * h + 16, 128 * l : 128 * l + 128]
            wire[2 * l + h] = rw[16 * h : 16 * h + 16, 128 * l : 128 * l + 128]
    pl.semaphore_wait(barrier, 23 + crossed)
    fzcopies = over_z(fwire, fz, fzs, fzr)
    zcopies = over_z(wire, zbuf, zs, zr)
    lcopies = [
        remote(
            lall.at[zl, y], lall.at[zl, y], ls.at[k - 1], lr.at[k - 1],
            device(y_=rem(y + k // 2, 4), zl_=rem(zl + k % 2, 2)),
        )
        for k in range(1, 8)
    ]

    for c in lcopies:
        c.start()

    fbcopies, bcopies = {}, {}

    def spread_flags(d):
        fbcopies[d] = spread_out(d, fz, fzr, fall, fbs, fbr)

    def spread_right(d):
        bcopies[d] = spread_out(d, zbuf, zr, rall, bs, br)

    spread_flags(0)
    spread_right(0)
    for c in inputs[8:]:
        c.wait()
    wf_ref[...] = wm_ref[...].astype(F32)
    for e in range(32):
        wec_ref[32 * e : 32 * e + 32, :] = wf_ref[pl.ds(e, 32, stride=32), :].astype(BF)
    dt_ref[...] = delta_ref[...].astype(F32).reshape(1024, 128).T.astype(BF)
    perm2_ref[...] = ones_where(
        ((rows >> 7) == ((cols >> 4) & 3)) & (((rows >> 4) & 7) == (cols >> 6)) & ((rows & 15) == (cols & 15))
    ).astype(BF)
    spread_flags(1)
    spread_flags(3)
    spread_right(1)
    spread_right(3)

    def product(l):
        tile_ref[...] = dot(wec_ref[256 * l : 256 * l + 256, :], dt_ref[...])

        def spread_pair(p, carry):
            lanes = pl.ds(pl.multiple_of(p * 128, 128), 128)
            for t in range(4):
                a, b = swap_halves(tile_ref[64 * t : 64 * t + 32, lanes], tile_ref[64 * t + 32 : 64 * t + 64, lanes])
                place = slice(128 * t, 128 * t + 128)
                draw_ref[pl.ds(pl.multiple_of(p * 64, 64), 32), place] = a.astype(BF)
                draw_ref[pl.ds(pl.multiple_of(p * 64 + 32, 32), 32), place] = b.astype(BF)
            return carry

        lax.fori_loop(0, 8, spread_pair, 0)
        part = dot(draw_ref[...], perm2_ref[...], 1, 1).astype(BF)
        for g in range(4):
            place = slice(256 * l + 128 * (g // 2), 256 * l + 128 * (g // 2) + 128)
            d_ref[g % 2, :, place] = part[:, 128 * g : 128 * g + 128]

    spread_flags(2)
    product(0)
    product(1)
    product(2)
    spread_right(2)
    product(3)

    for xs in range(4):
        for ys in range(4):
            landed(fall.at[0, 0, 0, 0], fbr.at[xs, ys])
    fcopy = remote(fall.at[core], fall.at[core], fcs.at[0], fcr.at[0], device(core_=other))
    fcopy.start()
    for c in lcopies:
        c.wait_recv()
    for b in range(8):
        for l in range(4):
            for h in range(2):
                left_ref[32 * b + 16 * h : 32 * b + 16 * h + 16, 128 * l : 128 * l + 128] = lall[b // 4, b % 4, 2 * l + h]
    fcopy.wait_recv()

    mi = jnp.concatenate([lall[b // 4, b % 4, 8] for b in range(8)], axis=1)
    mj = jnp.concatenate(
        [jnp.concatenate([fall[g % 2, g // 2, b // 4, b % 4] for b in range(8)], axis=1) for g in range(4)], axis=0
    )
    count = dot(mi, mj, 1, 1).astype(BF)
    lane = iota((64, 512), 1)
    spread = dot(count, ones_where(iota((64, 512), 0) == ((lane >> 7) * 16 + (lane & 15))).astype(BF))
    spread = 1.0 / (spread + 0.001)
    for g in range(4):
        rec_ref[g] = spread[:, 128 * g : 128 * g + 128]

    def scale(i, carry):
        here = pl.ds(pl.multiple_of(i * 32, 32), 32)
        for g in range(4):
            factor = jnp.broadcast_to(rec_ref[g, pl.ds(i, 1), :], (32, 128))
            for l in range(4):
                lanes = slice(256 * l + 128 * (g // 2), 256 * l + 128 * (g // 2) + 128)
                d_ref[g % 2, here, lanes] = (d_ref[g % 2, here, lanes].astype(F32) * factor).astype(BF)
        return carry

    lax.fori_loop(0, 16, scale, 0)

    part = dot(left_ref[...], d_ref[other]).astype(BF)
    for l in range(4):
        for g in range(2):
            lanes = slice(256 * l + 128 * g, 256 * l + 128 * g + 128)
            gsend[:, g, :, 2 * l : 2 * l + 2] = part[:, lanes].reshape(2, 4, 2, 16, 128)
    gcopies = []
    for n in range(2):
        half = rem(tzl + 1 + n, 2)
        c = remote(gsend.at[half], gcore.at[half], gcs.at[n], gcr.at[n], device(core_=other))
        c.start()
        gcopies.append(c)
    part = dot(left_ref[...], d_ref[core])
    for l in range(4):
        for g in range(2):
            lanes = slice(256 * l + 128 * g, 256 * l + 128 * g + 128)
            own_ref[:, g, :, 2 * l : 2 * l + 2] = part[:, lanes].reshape(2, 4, 2, 16, 128)

    gbcopies = []
    for n in range(2):
        half = rem(tzl + 1 + n, 2)
        gcopies[n].wait_recv()
        hsend[half] = (own_ref[half] + gcore[half].astype(F32)).astype(BF)
        for m in range(2):
            x_ = 2 * rem(div(x, 2) + 1 + n, 2) + rem(x + 1 + m, 2)
            hx, _ = twin(x_)
            for dy in (2, 1, 3, 0):
                y_ = rem(y + dy, 4)
                src = hsend.at[half, rem(hx, 2), y_]
                if n == 1 and m == 1 and dy == 0:
                    pltpu.make_async_copy(src, gx.at[x, y], gbr.at[x, y]).start()
                else:
                    c = remote(src, gx.at[x, y], gbs.at[n, m, dy], gbr.at[x, y], device(x_=x_, y_=y_))
                    c.start()
                    gbcopies.append(c)

    ccopies = []
    for n, (dx, dy) in enumerate(NEAR):
        xs, ys = rem(x + dx, 4), rem(y + dy, 4)
        gx_, gzl_ = twin(xs)
        block = rall.at[core, rem(gx_, 2), gzl_, ys]
        landed(block, br.at[xs, ys])
        c = remote(block, block, cs.at[n], cr.at[n], device(core_=other))
        c.start()
        ccopies.append(c)
    for c in ccopies:
        c.wait_recv()

    part = 0.0
    for g in range(2):
        for l in range(4):
            packed = jnp.concatenate(
                [rall[g, h, :, :, 2 * l : 2 * l + 2].reshape(256, 128) for h in range(2)], axis=1
            )
            part = part + dot(packed, d_ref[g, :, 256 * l : 256 * l + 256], 1, 1)
    part = part.astype(BF)
    for b in range(8):
        lsend[b % 4, b // 4] = part[32 * b : 32 * b + 32]
    glcopies = []
    for dy in (2, 1, 3):
        y_ = rem(y + dy, 4)
        c = remote(lsend.at[y_], lrecv.at[dy - 1], gls.at[dy], glr.at[dy], device(y_=y_))
        c.start()
        glcopies.append(c)

    def pair_part(l):
        packed = jnp.concatenate(
            [rall[g % 2, g // 2, :, :, 2 * l : 2 * l + 2].reshape(256, 128) for g in range(4)], axis=1
        )
        right_ref[...] = dot(packed, perm2_ref[...]).astype(BF)
        o = dot(left_ref[...], right_ref[...], 0, 0)
        for t in range(4):
            for p in range(8):
                a, b = swap_halves(
                    o[64 * p : 64 * p + 32, 128 * t : 128 * t + 128],
                    o[64 * p + 32 : 64 * p + 64, 128 * t : 128 * t + 128],
                )
                tile_ref[64 * t : 64 * t + 32, 128 * p : 128 * p + 128] = a
                tile_ref[64 * t + 32 : 64 * t + 64, 128 * p : 128 * p + 128] = b
        term = dot(wt_ref[:, 256 * l : 256 * l + 256], tile_ref[...].astype(BF))
        if l == 0:
            pt_ref[...] = term
        else:
            pt_ref[...] += term

    wt_ref[...] = wec_ref[...].astype(F32).T.astype(BF)
    pair_part(0)

    gzcopies = {}
    for d in (2, 1, 3, 0):
        t = rem(zh + d, 4)
        for s in range(4):
            landed(gx.at[s, t], gbr.at[s, t])
        total = gx[0, t].astype(F32) + gx[1, t].astype(F32) + gx[2, t].astype(F32) + gx[3, t].astype(F32)
        ksend[t] = total.astype(BF)
        c = remote(ksend.at[t], gz.at[zh], gzs.at[d], gzr.at[d], device(x_=tx, zl_=tzl, zh_=t))
        gzcopies[d] = c
        if d:
            c.start()
        else:

            @pl.when(crossed == 1)
            def _():
                c.start()

            @pl.when(crossed == 0)
            def _():
                pltpu.make_async_copy(ksend.at[zh], gz.at[zh], gzr.at[0]).start()

    for c in glcopies:
        c.wait_recv()
    dl = lsend[y].astype(F32) + lrecv[0].astype(F32) + lrecv[1].astype(F32) + lrecv[2].astype(F32)
    lsum[...] = dl.astype(BF)
    glcross = remote(lsum.at[1 - zl], lother, gls.at[0], glr.at[0], device(zl_=1 - zl))
    glcross.start()
    glcopies.append(glcross)
    pair_part(1)
    pair_part(2)
    pair_part(3)
    count = dot(count, ones_where(iota((64, 128), 0) == (iota((64, 128), 1) & 63)).astype(BF)) + 0.001
    low = iota((1, 128), 1) < 64
    denom = jnp.concatenate(
        [jnp.where(low, count[2 * p : 2 * p + 1], count[2 * p + 1 : 2 * p + 2]) for p in range(8)], axis=1
    )
    pair_ref[...] = (pt_ref[...] / denom).T.astype(BF).reshape(16, 64, 128)

    glcross.wait_recv()
    dl = (lsum[zl].astype(F32) + lother[...].astype(F32)) * mask1_ref[...]
    hi, lo = split(jnp.concatenate([dl[:, 32 * i : 32 * i + 32] for i in range(16)], axis=0))
    dnl_ref[...] = dot(hi, w1_ref[...]) + dot(lo, w1_ref[...])

    for d in (0, 1, 3, 2):
        t = rem(zh + 4 - d, 4)
        landed(gz.at[t], gzr.at[d])
    total = gz[0].astype(F32) + gz[1].astype(F32) + gz[2].astype(F32) + gz[3].astype(F32)
    dr = jnp.concatenate(
        [jnp.concatenate([total[2 * l], total[2 * l + 1]], axis=0) for l in range(4)], axis=1
    ) * mask2_ref[...]
    hi, lo = split(dr)
    dr = dot(hi, perm1_ref[...], 1, 1) + dot(lo, perm1_ref[...], 1, 1)

    hi, lo = split(jnp.concatenate([dr[:, 32 * i : 32 * i + 32] for i in range(16)], axis=0))
    dn = dnl_ref[...] + dot(hi, w2_ref[...]) + dot(lo, w2_ref[...])
    for i in range(16):
        for h in range(2):
            dn_ref[h, pl.ds(i, 32, stride=16), :] = dn[32 * i : 32 * i + 32, 128 * h : 128 * h + 128]
    dn = jnp.concatenate([dn_ref[0], dn_ref[1]], axis=1) * gain_ref[...]
    xhat = xhat_ref[...]
    dx = rstd_ref[:, 0:1] * (
        dn - jnp.mean(dn, axis=-1, keepdims=True) - xhat * jnp.mean(dn * xhat, axis=-1, keepdims=True)
    )
    grad_ref[...] = dx.astype(BF).reshape(32, 16, 256)

    for c in [fcopy] + lcopies + ccopies + gcopies + glcopies + gbcopies:
        c.wait_send()
    for d in (1, 2, 3):
        fzcopies[d].wait_send()
        zcopies[d].wait_send()
        gzcopies[d].wait_send()

    @pl.when(crossed == 1)
    def _():
        fzcopies[0].wait_send()
        zcopies[0].wait_send()
        gzcopies[0].wait_send()

    for d in range(4):
        for c in fbcopies[d][:3] + bcopies[d][:3]:
            c.wait_send()

        @pl.when(rem(zh + 4 - d, 4) != y)
        def _():
            fbcopies[d][3].wait_send()
            bcopies[d][3].wait_send()


def body(
    homolog_stack,
    presence_flags,
    normalizer_scaling,
    normalizer_offset,
    first_factor_matrix,
    first_factor_offset,
    second_factor_matrix,
    second_factor_offset,
    final_mapping_matrix,
    coupling_delta_cotangent,
):
    dma = pltpu.SemaphoreType.DMA
    vm = pltpu.VMEM
    whole = pl.BlockSpec(memory_space=pltpu.VMEM)
    far = pl.BlockSpec(memory_space=pltpu.HBM)
    return tuple(
        pl.pallas_call(
            kernel,
            out_shape=(
                vm((16, 64, 128), BF),
                vm((32, 16, 256), BF),
            ),
            in_specs=[far] * 10,
            out_specs=(whole, whole),
            scratch_shapes=[
                vm((32, 16, 256), BF),
                vm((16, 32), jnp.int32),
                vm((1, 256), F32),
                vm((1, 256), F32),
                vm((32, 256), BF),
                vm((1, 32), F32),
                vm((32, 256), BF),
                vm((1, 32), F32),
                vm((1024, 128), BF),
                vm((16, 64, 128), BF),
                dma((10,)),
                vm((512, 256), F32),
                vm((512, 128), F32),
                vm((512, 128), F32),
                vm((1024, 128), F32),
                vm((1024, 128), BF),
                vm((128, 1024), BF),
                vm((128, 1024), BF),
                vm((32, 512), F32),
                vm((32, 512), F32),
                vm((512, 512), BF),
                vm((512, 512), BF),
                vm((16, 128), BF),
                vm((4, 16, 128), BF),
                vm((2, 2, 2, 4, 16, 128), BF),
                vm((8, 16, 128), BF),
                vm((4, 8, 16, 128), BF),
                vm((2, 4, 9, 16, 128), BF),
                vm((2, 2, 2, 4, 8, 16, 128), BF),
                vm((256, 512), BF),
                vm((256, 512), BF),
                vm((256, 1024), F32),
                vm((512, 512), BF),
                vm((2, 512, 1024), BF),
                vm((4, 16, 128), F32),
                vm((128, 1024), F32),
                vm((2, 2, 4, 8, 16, 128), F32),
                vm((2, 2, 4, 8, 16, 128), BF),
                vm((2, 2, 4, 8, 16, 128), BF),
                vm((2, 2, 4, 8, 16, 128), BF),
                vm((4, 4, 8, 16, 128), BF),
                vm((4, 8, 16, 128), BF),
                vm((4, 8, 16, 128), BF),
                vm((4, 2, 32, 512), BF),
                vm((3, 2, 32, 512), BF),
                vm((2, 32, 512), BF),
                vm((32, 512), BF),
                vm((512, 256), F32),
                vm((2, 512, 128), F32),
                dma((4,)), dma((4,)),
                dma((4, 4)), dma((4, 4)),
                dma((1,)), dma((1,)),
                dma((4,)), dma((4,)),
                dma((4, 4)), dma((4, 4)),
                dma((16,)), dma((16,)),
                dma((7,)), dma((7,)),
                dma((2,)), dma((2,)),
                dma((2, 2, 4)), dma((4, 4)),
                dma((4,)), dma((4,)),
                dma((4,)), dma((4,)),
            ],
            compiler_params=pltpu.CompilerParams(
                collective_id=0, has_side_effects=True, vmem_limit_bytes=48 * 1024 * 1024
            ),
        )(
            *(
                pltpu.with_memory_space_constraint(a, pltpu.HBM)
                for a in (
                    homolog_stack,
                    presence_flags.T,
                    normalizer_scaling.reshape(1, 256),
                    normalizer_offset.reshape(1, 256),
                    first_factor_matrix.T,
                    first_factor_offset.reshape(1, 32),
                    second_factor_matrix.T,
                    second_factor_offset.reshape(1, 32),
                    final_mapping_matrix,
                    coupling_delta_cotangent,
                )
            )
        )
    )


def solution(mesh):
    return jax.shard_map(
        body,
        mesh=mesh,
        in_specs=(
            P("seq", "res", None),
            P("seq", "res"),
            P(),
            P(),
            P(),
            P(),
            P(),
            P(),
            P(),
            P("res", "seq", None),
        ),
        out_specs=(P("res", "seq", None), P("seq", "res", None)),
        check_vma=False,
    )
```

time: 52.2 us -> 47 us (0.900)
  Pallas kernels: 48.9 us -> 44.8 us
  local copies, waits for them, and re-layouts: 2.42 us -> 1.41 us
    pallas_call x1, Pallas kernels: 48.9 us -> 44.8 us  [body(): pl.pallas_call(kernel, out_shape=(vm((16, 64, 128), BF), vm((32, 16, 256)...]
    unnamed x4 -> x2, local copies, waits for them, and re-layouts: 2.42 us -> 1.41 us
where the time goes in v3:
time: 47 us; the launch traced here: 46.9 us
  Pallas kernels  44.8 us (95%)
  local copies, waits for them, and re-layouts  1.41 us (3%)
  between operations  0.64 us (1%)
    pallas_call x1, Pallas kernels, body(): pl.pallas_call(kernel, out_shape=(vm((16, 64, 128), BF), vm((32, 16, 256)...  44.8 us
    unnamed x2, local copies, waits for them, and re-layouts  1.41 us

profile of v3, /device:TPU:32, one launch (start us, length us, event | category | flops | bytes accessed | tf_op | source)
XLA Modules:
  0.0 46.9 jit_solution(13394844139883198832)
XLA Ops:
  0.6 44.8 %shard_map.113 = (bf16[16,64,128]{2,1,0:T(8,128)(2,1)S(1)}, bf16[32,16,256]{2,1,0:T(8,128)(2,1)S(1)}) custom-call(bf16[32,16,256]{2,1,0:T(8,128)(2,1)} %x_hbm.1, s32[16,32]{1,0:T(8,128)} %bitcast.9, f32[1,256]{1,0:T(1,128)} %bitcast.10, f32[1,256]{1,0:T(1,128)} %bitcast.11, bf16[32,256]{1,0:T(8,128)(2,1)} %bitcast.7, f32[1,32]{1,0:T(1,128)} %bitcast.12, ...), custom_call_target="tpu_custom_call" | custom-call | tf_op jit(solution)/shard_map/pallas_call | solution.py:476
  45.5 0.7 %copy.14 = bf16[16,64,128]{2,1,0:T(8,128)(2,1)} copy(bf16[16,64,128]{2,1,0:T(8,128)(2,1)S(1)} %get-tuple-element.2) | data formatting | bytes 524288
  46.2 0.7 %copy.15 = bf16[32,16,256]{2,1,0:T(8,128)(2,1)} copy(bf16[32,16,256]{2,1,0:T(8,128)(2,1)S(1)} %get-tuple-element.3) | data formatting | bytes 524288

commit v4 on v3

--- a/solution.py
+++ b/solution.py
@@ -56,6 +56,48 @@
     fzs, fzr, fbs, fbr, fcs, fcr, zs, zr, bs, br, cs, cr, ls, lr,
     gcs, gcr, gbs, gbr, gzs, gzr, gls, glr,
 ):
+    q = lax.axis_index("seq")
+    r = lax.axis_index("res")
+    y, zl = div(q, 2), rem(q, 2)
+    zh, x, core = div(r, 8), rem(div(r, 2), 4), rem(r, 2)
+    other = 1 - core
+
+    def device(x_=x, y_=y, zh_=zh, zl_=zl, core_=core):
+        return {"seq": y_ * 2 + zl_, "res": zh_ * 8 + x_ * 2 + core_}
+
+    def twin(x_):
+        m = rem(div(x_, 2) + zl, 2)
+        return x_ + m * (3 - 2 * x_), rem(zl + m, 2)
+
+    crossed = rem(div(x, 2) + zl, 2)
+    tx, tzl = twin(x)
+
+    def remote(src, dst, send, recv, where):
+        return pltpu.make_async_remote_copy(
+            src_ref=src, dst_ref=dst, send_sem=send, recv_sem=recv, device_id=where, device_id_type=MESH
+        )
+
+    def landed(ref, sem):
+        pltpu.make_async_copy(ref, ref, sem).wait()
+
+    barrier = pltpu.get_barrier_semaphore()
+
+    def greet(where):
+        pl.semaphore_signal(barrier, inc=1, device_id=where, device_id_type=MESH)
+
+    for d in (2, 1, 3):
+        greet(device(x_=tx, zl_=tzl, zh_=rem(zh + d, 4)))
+
+    @pl.when(crossed == 1)
+    def _():
+        greet(device(x_=tx, zl_=tzl))
+
+    for dx, dy in NEAR[:0:-1]:
+        greet(device(x_=rem(x + dx, 4), y_=rem(y + dy, 4)))
+    for dy in range(4):
+        greet(device(y_=rem(y + dy, 4), zl_=1 - zl))
+    greet(device(core_=other))
+
     inputs = [
         pltpu.make_async_copy(a, b, in_sem.at[n])
         for n, (a, b) in enumerate(
@@ -67,48 +109,6 @@
     ]
     for c in inputs:
         c.start()
-
-    q = lax.axis_index("seq")
-    r = lax.axis_index("res")
-    y, zl = div(q, 2), rem(q, 2)
-    zh, x, core = div(r, 8), rem(div(r, 2), 4), rem(r, 2)
-    other = 1 - core
-
-    def device(x_=x, y_=y, zh_=zh, zl_=zl, core_=core):
-        return {"seq": y_ * 2 + zl_, "res": zh_ * 8 + x_ * 2 + core_}
-
-    def twin(x_):
-        m = rem(div(x_, 2) + zl, 2)
-        return x_ + m * (3 - 2 * x_), rem(zl + m, 2)
-
-    crossed = rem(div(x, 2) + zl, 2)
-    tx, tzl = twin(x)
-
-    def remote(src, dst, send, recv, where):
-        return pltpu.make_async_remote_copy(
-            src_ref=src, dst_ref=dst, send_sem=send, recv_sem=recv, device_id=where, device_id_type=MESH
-        )
-
-    def landed(ref, sem):
-        pltpu.make_async_copy(ref, ref, sem).wait()
-
-    barrier = pltpu.get_barrier_semaphore()
-
-    def greet(where):
-        pl.semaphore_signal(barrier, inc=1, device_id=where, device_id_type=MESH)
-
-    for d in (2, 1, 3):
-        greet(device(x_=tx, zl_=tzl, zh_=rem(zh + d, 4)))
-
-    @pl.when(crossed == 1)
-    def _():
-        greet(device(x_=tx, zl_=tzl))
-
-    for dx, dy in NEAR[1:]:
-        greet(device(x_=rem(x + dx, 4), y_=rem(y + dy, 4)))
-    for dy in range(4):
-        greet(device(y_=rem(y + dy, 4), zl_=1 - zl))
-    greet(device(core_=other))
 
     inputs[1].wait()
     flags_t = flag_ref[...].astype(F32).astype(BF)
@@ -191,7 +191,7 @@
             lall.at[zl, y], lall.at[zl, y], ls.at[k - 1], lr.at[k - 1],
             device(y_=rem(y + k // 2, 4), zl_=rem(zl + k % 2, 2)),
         )
-        for k in range(1, 8)
+        for k in (5, 4, 3, 7, 2, 6, 1)
     ]
 
     for c in lcopies:
@@ -207,6 +207,30 @@
 
     spread_flags(0)
     spread_right(0)
+    spread_flags(1)
+    spread_flags(3)
+    spread_flags(2)
+    spread_right(1)
+    spread_right(3)
+
+    def product(l):
+        tile_ref[...] = dot(wec_ref[256 * l : 256 * l + 256, :], dt_ref[...])
+
+        def spread_pair(p, carry):
+            lanes = pl.ds(pl.multiple_of(p * 128, 128), 128)
+            for t in range(4):
+                a, b = swap_halves(tile_ref[64 * t : 64 * t + 32, lanes], tile_ref[64 * t + 32 : 64 * t + 64, lanes])
+                place = slice(128 * t, 128 * t + 128)
+                draw_ref[pl.ds(pl.multiple_of(p * 64, 64), 32), place] = a.astype(BF)
+                draw_ref[pl.ds(pl.multiple_of(p * 64 + 32, 32), 32), place] = b.astype(BF)
+            return carry
+
+        lax.fori_loop(0, 8, spread_pair, 0)
+        part = dot(draw_ref[...], perm2_ref[...], 1, 1).astype(BF)
+        for g in range(4):
+            place = slice(256 * l + 128 * (g // 2), 256 * l + 128 * (g // 2) + 128)
+            d_ref[g % 2, :, place] = part[:, 128 * g : 128 * g + 128]
+
     for c in inputs[8:]:
         c.wait()
     wf_ref[...] = wm_ref[...].astype(F32)
@@ -216,34 +240,10 @@
     perm2_ref[...] = ones_where(
         ((rows >> 7) == ((cols >> 4) & 3)) & (((rows >> 4) & 7) == (cols >> 6)) & ((rows & 15) == (cols & 15))
     ).astype(BF)
-    spread_flags(1)
-    spread_flags(3)
-    spread_right(1)
-    spread_right(3)
-
-    def product(l):
-        tile_ref[...] = dot(wec_ref[256 * l : 256 * l + 256, :], dt_ref[...])
-
-        def spread_pair(p, carry):
-            lanes = pl.ds(pl.multiple_of(p * 128, 128), 128)
-            for t in range(4):
-                a, b = swap_halves(tile_ref[64 * t : 64 * t + 32, lanes], tile_ref[64 * t + 32 : 64 * t + 64, lanes])
-                place = slice(128 * t, 128 * t + 128)
-                draw_ref[pl.ds(pl.multiple_of(p * 64, 64), 32), place] = a.astype(BF)
-                draw_ref[pl.ds(pl.multiple_of(p * 64 + 32, 32), 32), place] = b.astype(BF)
-            return carry
-
-        lax.fori_loop(0, 8, spread_pair, 0)
-        part = dot(draw_ref[...], perm2_ref[...], 1, 1).astype(BF)
-        for g in range(4):
-            place = slice(256 * l + 128 * (g // 2), 256 * l + 128 * (g // 2) + 128)
-            d_ref[g % 2, :, place] = part[:, 128 * g : 128 * g + 128]
-
-    spread_flags(2)
     product(0)
+    spread_right(2)
     product(1)
     product(2)
-    spread_right(2)
     product(3)
 
     for xs in range(4):
@@ -365,8 +365,6 @@
         else:
             pt_ref[...] += term
 
-    wt_ref[...] = wec_ref[...].astype(F32).T.astype(BF)
-    pair_part(0)
 
     gzcopies = {}
     for d in (2, 1, 3, 0):
@@ -389,6 +387,8 @@
             def _():
                 pltpu.make_async_copy(ksend.at[zh], gz.at[zh], gzr.at[0]).start()
 
+    wt_ref[...] = wec_ref[...].astype(F32).T.astype(BF)
+    pair_part(0)
     for c in glcopies:
         c.wait_recv()
     dl = lsend[y].astype(F32) + lrecv[0].astype(F32) + lrecv[1].astype(F32) + lrecv[2].astype(F32)

time: 47 us -> 46.4 us (0.987)
  Pallas kernels: 44.8 us -> 44.1 us
    pallas_call x1, Pallas kernels: 44.8 us -> 44.1 us  [body(): pl.pallas_call(kernel, out_shape=(vm((16, 64, 128), BF), vm((32, 16, 256)...]
where the time goes in v4:
time: 46.4 us; the launch traced here: 46.2 us
  Pallas kernels  44.1 us (95%)
  local copies, waits for them, and re-layouts  1.41 us (3%)
  between operations  0.64 us (1%)
    pallas_call x1, Pallas kernels, body(): pl.pallas_call(kernel, out_shape=(vm((16, 64, 128), BF), vm((32, 16, 256)...  44.1 us
    unnamed x2, local copies, waits for them, and re-layouts  1.41 us

profile of v4, /device:TPU:32, one launch (start us, length us, event | category | flops | bytes accessed | tf_op | source)
XLA Modules:
  0.0 46.2 jit_solution(2373259562714081649)
XLA Ops:
  0.6 44.1 %shard_map.113 = (bf16[16,64,128]{2,1,0:T(8,128)(2,1)S(1)}, bf16[32,16,256]{2,1,0:T(8,128)(2,1)S(1)}) custom-call(bf16[32,16,256]{2,1,0:T(8,128)(2,1)} %x_hbm.1, s32[16,32]{1,0:T(8,128)} %bitcast.9, f32[1,256]{1,0:T(1,128)} %bitcast.10, f32[1,256]{1,0:T(1,128)} %bitcast.11, bf16[32,256]{1,0:T(8,128)(2,1)} %bitcast.7, f32[1,32]{1,0:T(1,128)} %bitcast.12, ...), custom_call_target="tpu_custom_call" | custom-call | tf_op jit(solution)/shard_map/pallas_call | solution.py:476
  44.8 0.7 %copy.14 = bf16[16,64,128]{2,1,0:T(8,128)(2,1)} copy(bf16[16,64,128]{2,1,0:T(8,128)(2,1)S(1)} %get-tuple-element.2) | data formatting | bytes 524288
  45.5 0.7 %copy.15 = bf16[32,16,256]{2,1,0:T(8,128)(2,1)} copy(bf16[32,16,256]{2,1,0:T(8,128)(2,1)S(1)} %get-tuple-element.3) | data formatting | bytes 524288

commit v5 on v4

--- a/solution.py
+++ b/solution.py
@@ -191,7 +191,7 @@
             lall.at[zl, y], lall.at[zl, y], ls.at[k - 1], lr.at[k - 1],
             device(y_=rem(y + k // 2, 4), zl_=rem(zl + k % 2, 2)),
         )
-        for k in (5, 4, 3, 7, 2, 6, 1)
+        for k in (4, 2, 6, 5, 3, 7, 1)
     ]
 
     for c in lcopies:
@@ -304,7 +304,7 @@
         gcopies[n].wait_recv()
         hsend[half] = (own_ref[half] + gcore[half].astype(F32)).astype(BF)
         for m in range(2):
-            x_ = 2 * rem(div(x, 2) + 1 + n, 2) + rem(x + 1 + m, 2)
+            x_ = 2 * rem(div(x, 2) + 1 + n, 2) + rem(x + n + m, 2)
             hx, _ = twin(x_)
             for dy in (2, 1, 3, 0):
                 y_ = rem(y + dy, 4)

time: 46.4 us -> 46.2 us (level)
  no operation moved by 1% of the time
where the time goes in v5:
time: 46.2 us; the launch traced here: 46.1 us
  Pallas kernels  44.1 us (95%)
  local copies, waits for them, and re-layouts  1.41 us (3%)
  between operations  0.64 us (1%)
    pallas_call x1, Pallas kernels, body(): pl.pallas_call(kernel, out_shape=(vm((16, 64, 128), BF), vm((32, 16, 256)...  44.1 us
    unnamed x2, local copies, waits for them, and re-layouts  1.41 us

profile of v5, /device:TPU:32, one launch (start us, length us, event | category | flops | bytes accessed | tf_op | source)
XLA Modules:
  0.0 46.1 jit_solution(18241071295043234105)
XLA Ops:
  0.6 44.1 %shard_map.113 = (bf16[16,64,128]{2,1,0:T(8,128)(2,1)S(1)}, bf16[32,16,256]{2,1,0:T(8,128)(2,1)S(1)}) custom-call(bf16[32,16,256]{2,1,0:T(8,128)(2,1)} %x_hbm.1, s32[16,32]{1,0:T(8,128)} %bitcast.9, f32[1,256]{1,0:T(1,128)} %bitcast.10, f32[1,256]{1,0:T(1,128)} %bitcast.11, bf16[32,256]{1,0:T(8,128)(2,1)} %bitcast.7, f32[1,32]{1,0:T(1,128)} %bitcast.12, ...), custom_call_target="tpu_custom_call" | custom-call | tf_op jit(solution)/shard_map/pallas_call | solution.py:476
  44.7 0.7 %copy.14 = bf16[16,64,128]{2,1,0:T(8,128)(2,1)} copy(bf16[16,64,128]{2,1,0:T(8,128)(2,1)S(1)} %get-tuple-element.2) | data formatting | bytes 524288
  45.4 0.7 %copy.15 = bf16[32,16,256]{2,1,0:T(8,128)(2,1)} copy(bf16[32,16,256]{2,1,0:T(8,128)(2,1)S(1)} %get-tuple-element.3) | data formatting | bytes 524288
